TPU v7x, 32 devices: a whole 2x2x4 slice. The times are simulated.
32 devices in a mesh: clip: 2 (over y), tm: 4 (over z), head: 2 (over x), sub: 2 (over core).
Axes of the slice: x: 2, y: 2, z: 4, core: 2. Of those that a mesh axis runs over, the one named last changes fastest.
Arguments:
- queries: bfloat16 [8, 256, 3072], P(('clip', 'tm'), None, ('head', 'sub')), parts along dimension 0, may hold values from -6 to 6, as said below
- keys: bfloat16 [8, 256, 3072], P(('clip', 'tm'), None, ('head', 'sub')), parts along dimension 0, may hold values from -6 to 6, as said below
- values: bfloat16 [8, 256, 3072], P(('clip', 'tm'), None, ('head', 'sub')), parts along dimension 0, may hold values from -6 to 6
- band_table: int32 [4, 4], replicated, may hold values from 0 to 3, as said below
- windows: int32 [7], replicated, may hold values from 1 to 128, as said below
- out_weight: bfloat16 [3072, 3072], P(('head', 'sub')), may hold values from -0.109375 to 0.109375
Outputs:
- mixed: bfloat16 [8, 256, 3072], P(('clip', 'tm'), ('head', 'sub')), parts along dimension 0
There are 2 independent parts, one for each index of `clip`. A program takes and returns all parts, laid end to end along the dimension named above; an argument that names none is the same for every part. Nothing has to cross between parts.
Inputs may be any that keep to these rules, and one draw needn't show every extreme that they name: `queries`: entries of normal law within the range; some rows may be aligned with some key rows. `keys`: entries of normal law within the range; some rows may be aligned with some query rows. `band_table`: Symmetric; 0 exactly on the diagonal; off the diagonal, for frames at distance d it is floor(log2 d) + 1 or one more, never above 6; the pair of frames 0 and 3 takes the one more (up to 6). windows[0] = 128; for k >= 1, windows[k] lies between max(1, 64 // 2**k) and max(that + 1, 128 // 2**k + 1) - 1.
All inputs are finite; a program needn't handle non-finite values.
Results may differ from a plain program's by a relative error of at most 0.015.
Values may be sent and summed in bfloat16 or wider, within the bound.
No kernel may reach another device: no remote copies, remote signals or barrier semaphores. Data moves between devices by JAX's collectives and lax.ppermute only.
A program may use at most 64 MiB of HBM per device.

v0:
```python
import jax
import jax.numpy as jnp
from jax import lax
from jax.sharding import PartitionSpec as P

HEAD = 128


def local(queries, keys, values, band_table, windows, out_weight):
    frames, length, width = queries.shape
    heads = width // HEAD
    scale = HEAD ** (-0.5)
    here = lax.axis_index("tm") * frames
    query = queries[0].reshape(length, heads, HEAD)
    places = lax.iota(jnp.int32, length)
    gap = jnp.abs(places[:, None] - places[None, :])

    def absorb(carry, key_frame, value_frame, frame, usable):
        peak, total, numer = carry
        reach = windows[band_table[here, frame]]
        allowed = (gap <= reach)[None] & usable
        scores = (
            jnp.einsum(
                "phd,qhd->hpq",
                query,
                key_frame.reshape(length, heads, HEAD),
                preferred_element_type=jnp.float32,
            )
            * scale
        )
        masked = jnp.where(allowed, scores, jnp.float32(-1e30))
        top = jnp.maximum(peak, jnp.max(masked, axis=-1))
        weights = jnp.where(allowed, jnp.exp(scores - top[:, :, None]), jnp.float32(0.0))
        shrink = jnp.exp(peak - top)
        total = total * shrink + jnp.sum(weights, axis=-1)
        added = jnp.einsum(
            "hpq,qhd->phd",
            weights.astype(jnp.bfloat16),
            value_frame.reshape(length, heads, HEAD),
            preferred_element_type=jnp.float32,
        )
        numer = numer * jnp.transpose(shrink)[:, :, None] + added
        return (top, total, numer)

    carry = (
        jnp.full((heads, length), -1e30, jnp.float32),
        jnp.zeros((heads, length), jnp.float32),
        jnp.zeros((length, heads, HEAD), jnp.float32),
    )
    skipped = -1
    state = carry
    key_part = lax.all_gather(keys, "tm", axis=0, tiled=True)
    value_part = lax.all_gather(values, "tm", axis=0, tiled=True)

    def advance(inner, item):
        key_frame, value_frame, offset = item
        usable = jnp.abs(offset - here) > skipped
        return (absorb(inner, key_frame, value_frame, offset, usable), None)

    state, unused = lax.scan(
        advance, state, (key_part, value_part, lax.iota(jnp.int32, key_part.shape[0]))
    )
    carry = state
    peak, total, numer = carry
    attended = (
        (numer / jnp.transpose(total)[:, :, None]).astype(jnp.bfloat16).reshape(length, width)
    )
    mixed = lax.psum_scatter(
        jnp.dot(attended, out_weight, preferred_element_type=jnp.float32).astype(jnp.bfloat16),
        ("head", "sub"),
        scatter_dimension=0,
        tiled=True,
    )
    return mixed[None]


def solution(mesh):
    return jax.shard_map(
        local,
        mesh=mesh,
        in_specs=(
            P(("clip", "tm"), None, ("head", "sub")),
            P(("clip", "tm"), None, ("head", "sub")),
            P(("clip", "tm"), None, ("head", "sub")),
            P(),
            P(),
            P(("head", "sub"), None),
        ),
        out_specs=P(("clip", "tm"), ("head", "sub"), None),
        check_vma=False,
    )
```

profile of v0, /device:TPU:0, one launch (start us, length us, event | category | flops | bytes accessed | tf_op | source)
XLA Modules:
  0.0 170.2 jit_solution(7781933475861130219)
XLA Ops:
  6.5 0.0 copy-start
  6.5 0.0 all-gather.3.cloned.1.call-start
  6.5 0.7 all-gather.3.cloned.1.call-update
  7.3 0.0 all-gather.5.cloned.1.call-start
  7.3 0.7 all-gather.5.cloned.1.call-update
  8.0 0.0 reduce-scatter.2.cloned.1.call-start
  8.1 1.2 copy.17
  9.3 0.9 copy.19
  10.2 38.6 %all-gather.3.cloned.1.call-done = bf16[4,256,768]{2,1,0:T(8,128)(2,1)} async-done(((bf16[1,256,768]{2,1,0:T(8,128)(2,1)}), bf16[4,256,768]{2,1,0:T(8,128)(2,1)}) %all-gather.3.cloned.1.call-update) | async-done | bytes 1572880 | tf_op jit(solution)/shard_map/all_gather | solution.py:52
  48.8 37.6 %all-gather.5.cloned.1.call-done = bf16[4,256,768]{2,1,0:T(8,128)(2,1)} async-done(((bf16[1,256,768]{2,1,0:T(8,128)(2,1)}), bf16[4,256,768]{2,1,0:T(8,128)(2,1)}) %all-gather.5.cloned.1.call-update) | async-done | bytes 1572880 | tf_op jit(solution)/shard_map/all_gather | solution.py:53
  86.3 0.0 copy-done
  86.3 45.1 %while.17 = (s32[]{:T(128)}, f32[6,256]{1,0:T(8,128)S(1)}, f32[6,256]{1,0:T(8,128)S(1)}, f32[256,6,128]{0,2,1:T(8,128)S(1)}, s32[4]{0:T(128)S(1)}, /*index=5*/s3...) while((s32[]{:T(128)}, f32[6,256]{1,0:T(8,128)S(1)}, ...), condition=%wide.region_3.4_spmd.clone, body=%wide.region_0.3_spmd.clone.sunk | while | flops 205726720 | bytes 10977591 | solution.py:60
  86.3 0.6 dynamic_slice.39
  88.6 1.3 dynamic_slice.40
  91.8 0.6 dynamic_slice.41
  93.0 0.7 fusion.35
  93.7 1.2 constant_dynamic-slice_fusion.3
  94.9 0.2 copy.27
  95.1 1.5 fusion.36
  96.6 0.2 copy.28
  96.7 0.5 fusion.40
  97.3 0.3 fusion.38
  97.6 0.6 dynamic_slice.39
  99.9 1.3 dynamic_slice.40
  103.1 0.6 dynamic_slice.41
  104.3 0.7 fusion.35
  105.0 1.2 constant_dynamic-slice_fusion.3
  106.2 0.2 copy.27
  106.4 1.5 fusion.36
  107.8 0.2 copy.28
  108.0 0.5 fusion.40
  108.5 0.3 fusion.38
  108.9 0.6 dynamic_slice.39
  111.2 1.3 dynamic_slice.40
  114.4 0.6 dynamic_slice.41
  115.6 0.7 fusion.35
  116.3 1.2 constant_dynamic-slice_fusion.3
  117.5 0.2 copy.27
  117.6 1.4 fusion.36
  119.1 0.2 copy.28
  119.3 0.5 fusion.40
  119.8 0.3 fusion.38
  120.2 0.6 dynamic_slice.39
  122.4 1.3 dynamic_slice.40
  125.7 0.6 dynamic_slice.41
  126.9 0.7 fusion.35
  127.6 1.2 constant_dynamic-slice_fusion.3
  128.8 0.2 copy.27
  128.9 1.4 fusion.36
  130.4 0.2 copy.28
  130.6 0.5 fusion.40
  131.1 0.3 fusion.38
  131.4 0.1 divide_convert_fusion
  131.5 4.9 %convolution_convert_fusion = bf16[256,3072]{1,0:T(8,128)(2,1)} fusion(bf16[256,768]{0,1:T(8,128)(2,1)S(1)} %bitcast.62, bf16[768,3072]{1,0:T(8,128)(2,1)} %param.13), kind=kOutput, calls=%fused_computation.25 | convolution fusion | flops 1208745984 | bytes 6684672 | tf_op jit(solution)/shard_map/dot_general | solution.py:69
  136.4 0.0 reduce-scatter.2.cloned.1.call-update
  136.5 27.2 %reduce-scatter.2.cloned.1.call-done = bf16[64,3072]{1,0:T(8,128)(2,1)} async-done(((bf16[256,3072]{1,0:T(8,128)(2,1)}), bf16[64,3072]{1,0:T(8,128)(2,1)}) %reduce-scatter.2.cloned.1.call-update) | async-done | bytes 393232 | tf_op jit(solution)/shard_map/reduce_scatter | solution.py:68
  (16 shorter events, 0.1 us)
Async XLA Ops:
  6.5 79.8 %copy-start = (s32[7]{0:T(128)S(1)}, s32[7]{0:T(128)}, u32[]{:S(2)}) copy-start(s32[7]{0:T(128)} %param.12) | copy-start | bytes 88
  6.5 42.2 %all-gather.3.cloned.1.call-start = ((), (), s32[]{:S(2)}) async-start(), calls=%async_computation.1 | async-start | bytes 1966080 | tf_op jit(solution)/shard_map/all_gather | solution.py:52
  7.3 79.0 %all-gather.5.cloned.1.call-start = ((), (), s32[]{:S(2)}) async-start(), calls=%async_computation.2 | async-start | bytes 1966080 | tf_op jit(solution)/shard_map/all_gather | solution.py:53
  8.0 155.6 %reduce-scatter.2.cloned.1.call-start = ((), (), s32[]{:S(2)}) async-start(), calls=%async_computation.3 | async-start | bytes 1966080 | tf_op jit(solution)/shard_map/reduce_scatter | solution.py:68
Sparse Core Ops, SparseCore 0:
  8.9 39.7 all-gather.2
  50.3 35.9 all-gather.4
  136.6 27.0 reduce-scatter.1
where the time goes:
time: 171 us; the launch traced here: 170 us
  waiting for transfers between devices  105 us (61%)
  local copies, waits for them, and re-layouts  18.4 us (11%)
  loops' own time  16.9 us (10%)
  between operations  13.2 us (8%)
  matrix products  12.8 us (7%)
  other arithmetic  4.12 us (2%)
    all_gather x1, waiting for transfers between devices, local(): key_part = lax.all_gather(keys, 'tm', axis=0, tiled=True)  38.6 us
    all_gather x1, waiting for transfers between devices, local(): value_part = lax.all_gather(values, 'tm', axis=0, tiled=True)  37.6 us
    reduce_scatter x1, waiting for transfers between devices, local(): lax.psum_scatter(jnp.dot(attended, out_weight, preferred_element_type=jnp...  27.2 us
    another operation x1, loops' own time, local(): lax.scan(advance, state, (key_part, value_part, lax.iota(jnp.int32, key_p...  16.9 us
    dynamic_slice x16, local copies, waits for them, and re-layouts, local(): lax.scan(advance, state, (key_part, value_part, lax.iota(jnp.int32, key_p...  8.4 us
    dynamic_slice x8, local copies, waits for them, and re-layouts, absorb(): reach = windows[band_table[here, frame]]  7.86 us
    dot_general x4, matrix products, absorb(): jnp.einsum('phd,qhd->hpq', query, key_frame.reshape(length, heads, HEAD),...  5.8 us
    dot_general x1, matrix products, local(): jnp.dot(attended, out_weight, preferred_element_type=jnp.float32)  4.92 us
  transfers between devices with their start and end apart: 3, of which 3 were waited for; matrix products, arithmetic and copies ran while one was open for 1% of the time, Pallas kernels for 0%

commit v1 on v0

--- a/solution.py
+++ b/solution.py
@@ -1,12 +1,20 @@
+import functools
+
 import jax
 import jax.numpy as jnp
 from jax import lax
+from jax.experimental import pallas as pl
+from jax.experimental.pallas import tpu as pltpu
 from jax.sharding import PartitionSpec as P
 
 HEAD = 128
-
-
-def local(queries, keys, values, band_table, windows, out_weight):
+ANY = pl.BlockSpec(memory_space=pl.ANY)
+VMEM = pl.BlockSpec(memory_space=pltpu.VMEM)
+SMEM = pl.BlockSpec(memory_space=pltpu.SMEM)
+CHUNKS = 2
+
+
+def gathered(queries, keys, values, band_table, windows, out_weight):
     frames, length, width = queries.shape
     heads = width // HEAD
     scale = HEAD ** (-0.5)
@@ -15,10 +23,10 @@
     places = lax.iota(jnp.int32, length)
     gap = jnp.abs(places[:, None] - places[None, :])
 
-    def absorb(carry, key_frame, value_frame, frame, usable):
+    def absorb(carry, key_frame, value_frame, frame):
         peak, total, numer = carry
         reach = windows[band_table[here, frame]]
-        allowed = (gap <= reach)[None] & usable
+        allowed = (gap <= reach)[None]
         scores = (
             jnp.einsum(
                 "phd,qhd->hpq",
@@ -47,21 +55,16 @@
         jnp.zeros((heads, length), jnp.float32),
         jnp.zeros((length, heads, HEAD), jnp.float32),
     )
-    skipped = -1
-    state = carry
     key_part = lax.all_gather(keys, "tm", axis=0, tiled=True)
     value_part = lax.all_gather(values, "tm", axis=0, tiled=True)
 
     def advance(inner, item):
-        key_frame, value_frame, offset = item
-        usable = jnp.abs(offset - here) > skipped
-        return (absorb(inner, key_frame, value_frame, offset, usable), None)
-
-    state, unused = lax.scan(
-        advance, state, (key_part, value_part, lax.iota(jnp.int32, key_part.shape[0]))
-    )
-    carry = state
-    peak, total, numer = carry
+        return (absorb(inner, *item), None)
+
+    state, _ = lax.scan(
+        advance, carry, (key_part, value_part, lax.iota(jnp.int32, key_part.shape[0]))
+    )
+    _, total, numer = state
     attended = (
         (numer / jnp.transpose(total)[:, :, None]).astype(jnp.bfloat16).reshape(length, width)
     )
@@ -74,7 +77,254 @@
     return mixed[None]
 
 
+def run_copies(copies, sem):
+    started = [pltpu.make_async_copy(s, d, sem.at[i]) for i, (s, d) in enumerate(copies)]
+    for copy in started:
+        copy.start()
+    for copy in started:
+        copy.wait()
+
+
+def pack_kernel(n, cores, tokens, q_ref, k_ref, v_ref, *rest):
+    kv_out, q_out, sem = rest[:n], rest[n : 2 * n], rest[2 * n]
+    z = lax.axis_index("tm")
+    wide = kv_out[0].shape[2]
+    half = kv_out[0].shape[1]
+    copies = []
+    for r in range(n):
+        t = z ^ r
+        cols = pl.ds(pl.multiple_of((t // cores) * wide, wide), wide)
+        b = t % cores
+        rows = pl.ds(pl.multiple_of(b * half, half), half)
+        copies.append((k_ref.at[0, rows, cols], kv_out[r].at[0]))
+        copies.append((v_ref.at[0, rows, cols], kv_out[r].at[1]))
+        for x in range(half // tokens):
+            place = pl.ds(pl.multiple_of((x * cores + b) * tokens, tokens), tokens)
+            copies.append((q_ref.at[0, place, cols], q_out[r].at[pl.ds(x * tokens, tokens)]))
+    run_copies(copies, sem)
+
+
+def bias_kernel(n, cores, tokens, band_ref, reach_ref, _, bias_ref):
+    z, c = lax.axis_index("tm"), lax.axis_index("sub")
+    length = bias_ref.shape[1] // n
+    half = length // cores
+    t = (z % (n // cores)) * cores + c
+    row = lax.broadcasted_iota(jnp.int32, (half, length), 0)
+    key = lax.broadcasted_iota(jnp.int32, (half, length), 1)
+    place = (row // tokens * cores + c) * tokens + row % tokens
+    key_place = jnp.where(key < half, key + c * half, key - half + (1 - c) * half)
+    gap = jnp.abs(place - key_place)
+    for r in range(n):
+        for s in range(n):
+            reach = reach_ref[band_ref[t ^ r, t ^ s]]
+            bias_ref[r * half : (r + 1) * half, s * length : (s + 1) * length] = jnp.where(
+                gap <= reach, jnp.float32(0.0), jnp.float32(-1e30)
+            )
+
+
+def attend_kernel(n, cores, tokens, first, count, bias_ref, *rest):
+    own, other, query = rest[:n], rest[n : 2 * n], rest[2 * n : 3 * n]
+    outs = rest[3 * n : 4 * n]
+    s_all, p_all, t_all, o_all, sem = rest[4 * n :]
+    z, c = lax.axis_index("tm"), lax.axis_index("sub")
+    half = own[0].shape[1]
+    heads = own[0].shape[2] // HEAD
+    length = half * cores
+    blocks = half // tokens
+    rows = blocks * count
+    t = (z % (n // cores)) * cores + c
+    rate = jnp.float32(HEAD ** (-0.5) * 1.4426950408889634)
+    places = [
+        (r, x, (r * blocks + x) * count) for r in range(n) for x in range(blocks)
+    ]
+    for h in range(heads):
+        cols = slice(h * HEAD, (h + 1) * HEAD)
+        slot = h % 2
+        q = jnp.concatenate(
+            [query[r][x * tokens + first : x * tokens + first + count, cols] for r, x, _ in places]
+        )
+        for s in range(n):
+            k = jnp.concatenate([own[s][0, :, cols], other[s ^ 1][0, :, cols]])
+            s_all[slot, :, s * length : (s + 1) * length] = lax.dot_general(
+                q, k, (((1,), (1,)), ((), ())), preferred_element_type=jnp.float32
+            )
+        for r, x, at in places:
+            base = r * half + x * tokens + first
+            for step in range(0, count, 16):
+                lines = slice(at + step, at + step + 16)
+                parts = [
+                    s_all[slot, lines, g : g + 128]
+                    + bias_ref[base + step : base + step + 16, g : g + 128]
+                    for g in range(0, n * length, 128)
+                ]
+                top = jnp.max(functools.reduce(jnp.maximum, parts), axis=1, keepdims=True)
+                weights = [jnp.exp2((part - top) * rate) for part in parts]
+                total = jnp.sum(functools.reduce(jnp.add, weights), axis=1, keepdims=True)
+                t_all[slot, lines, :] = jnp.broadcast_to(1.0 / total, (16, HEAD))
+                for g, weight in enumerate(weights):
+                    p_all[slot, lines, g * 128 : (g + 1) * 128] = weight.astype(jnp.bfloat16)
+        numer = 0.0
+        for s in range(n):
+            v = jnp.concatenate([own[s][1, :, cols], other[s ^ 1][1, :, cols]])
+            numer += jnp.dot(
+                p_all[slot, :, s * length : (s + 1) * length], v,
+                preferred_element_type=jnp.float32,
+            )
+        result = (numer * t_all[slot]).astype(jnp.bfloat16)
+        for r in range(n):
+            o_all[r, :, cols] = result[r * rows : (r + 1) * rows]
+    run_copies([(o_all.at[t ^ z ^ k], outs[k]) for k in range(n)], sem)
+
+
+def project_kernel(n, cores, own_w, other_w, *rest):
+    parts = rest[:n]
+    keep_ref, send_ref, a_all, sem = rest[n:]
+    z, c, x = lax.axis_index("tm"), lax.axis_index("sub"), lax.axis_index("head")
+    count = keep_ref.shape[0]
+    copies = []
+    for k in range(n):
+        for b in range(2):
+            at = pl.ds(pl.multiple_of((b ^ 1 ^ x) * count, count), count)
+            copies.append((parts[k].at[at], a_all.at[z ^ k, pl.ds(b * count, count)]))
+    run_copies(copies, sem)
+    per = n // cores
+    wide = a_all.shape[2]
+    total = 0.0
+    for w_ref, core in ((own_w, c), (other_w, 1 - c)):
+        for g in range(per):
+            total += jnp.dot(
+                a_all[core * per + g], w_ref[g * wide : (g + 1) * wide, :],
+                preferred_element_type=jnp.float32,
+            )
+    send_ref[...] = total[:count].astype(send_ref.dtype)
+    keep_ref[...] = total[count:]
+
+
+def add_kernel(chunks, *refs):
+    out_ref = refs[-1]
+    for a in range(chunks):
+        keep, got = refs[2 * a], refs[2 * a + 1]
+        count = keep.shape[0]
+        out_ref[0, a * count : (a + 1) * count] = (
+            keep[...] + got[...].astype(jnp.float32)
+        ).astype(out_ref.dtype)
+
+
+def swapped(x, axis):
+    return lax.ppermute(x, axis, [(0, 1), (1, 0)])
+
+
+def spread(n, cores, queries, keys, values, band_table, windows, out_weight):
+    _, length, width = queries.shape
+    depth, model = out_weight.shape
+    wide = width * cores // n
+    half = length // cores
+    tokens = half // 2
+    bf16 = queries.dtype
+
+    packed = pl.pallas_call(
+        functools.partial(pack_kernel, n, cores, tokens),
+        out_shape=[jax.ShapeDtypeStruct((2, half, wide), bf16)] * n
+        + [jax.ShapeDtypeStruct((half, wide), bf16)] * n,
+        in_specs=[ANY] * 3,
+        out_specs=[VMEM] * (2 * n),
+        scratch_shapes=[pltpu.SemaphoreType.DMA((4 * n,))],
+        compiler_params=pltpu.CompilerParams(vmem_limit_bytes=4 * 2**20),
+        name="pack",
+    )(queries, keys, values)
+
+    per = n // cores
+    rounds = [
+        [
+            (z * cores + c, (c * per + (z ^ r) // cores) * cores + (z ^ r) % cores)
+            for z in range(n)
+            for c in range(cores)
+        ]
+        for r in range(n)
+    ]
+    own = [lax.ppermute(packed[r], ("tm", "sub"), rounds[r]) for r in range(n)]
+    query = []
+    for r in range(n):
+        block, _ = lax.optimization_barrier((packed[n + r], own[(r + 1) // 2]))
+        query.append(lax.ppermute(block, ("tm", "sub"), rounds[r]))
+    other = [swapped(block, "sub") for block in own]
+
+    weight, _ = lax.optimization_barrier((out_weight, own[1]))
+    other_weight = swapped(weight, "sub")
+    bias = pl.pallas_call(
+        functools.partial(bias_kernel, n, cores, tokens),
+        out_shape=jax.ShapeDtypeStruct((n * half, n * length), jnp.float32),
+        in_specs=[SMEM, SMEM, ANY],
+        out_specs=VMEM,
+        compiler_params=pltpu.CompilerParams(vmem_limit_bytes=4 * 2**20),
+        name="bias",
+    )(band_table, windows, packed[0])
+
+    count = tokens // CHUNKS
+    rows = 2 * count
+    sums = []
+    for a in range(CHUNKS):
+        outs = pl.pallas_call(
+            functools.partial(attend_kernel, n, cores, tokens, a * count, count),
+            out_shape=[jax.ShapeDtypeStruct((rows, wide), bf16)] * n,
+            in_specs=[VMEM] * (1 + 3 * n),
+            out_specs=[VMEM] * n,
+            scratch_shapes=[
+                pltpu.VMEM((2, n * rows, n * length), jnp.float32),
+                pltpu.VMEM((2, n * rows, n * length), bf16),
+                pltpu.VMEM((2, n * rows, HEAD), jnp.float32),
+                pltpu.VMEM((n, rows, wide), bf16),
+                pltpu.SemaphoreType.DMA((n,)),
+            ],
+            compiler_params=pltpu.CompilerParams(vmem_limit_bytes=24 * 2**20),
+            name="attend",
+        )(bias, *own, *other, *query)
+        parts = [outs[0]] + [
+            lax.ppermute(outs[k], "tm", [(z, z ^ k) for z in range(n)]) for k in range(1, n)
+        ]
+        keep, send = pl.pallas_call(
+            functools.partial(project_kernel, n, cores),
+            out_shape=[
+                jax.ShapeDtypeStruct((count, model), jnp.float32),
+                jax.ShapeDtypeStruct((count, model), bf16),
+            ],
+            in_specs=[VMEM] * (2 + n),
+            out_specs=[VMEM] * 2,
+            scratch_shapes=[
+                pltpu.VMEM((n, rows, wide), bf16),
+                pltpu.SemaphoreType.DMA((2 * n,)),
+            ],
+            compiler_params=pltpu.CompilerParams(vmem_limit_bytes=24 * 2**20),
+            name="project",
+        )(out_weight, other_weight, *parts)
+        sums += [keep, swapped(send, "head")]
+    return pl.pallas_call(
+        functools.partial(add_kernel, CHUNKS),
+        out_shape=jax.ShapeDtypeStruct((1, tokens, model), bf16),
+        in_specs=[VMEM] * (2 * CHUNKS),
+        out_specs=VMEM,
+        compiler_params=pltpu.CompilerParams(vmem_limit_bytes=4 * 2**20),
+        name="add",
+    )(*sums)
+
+
 def solution(mesh):
+    n, cores, xs = mesh.shape["tm"], mesh.shape["sub"], mesh.shape["head"]
+
+    def local(queries, keys, values, band_table, windows, out_weight):
+        frames, length, width = queries.shape
+        fits = (
+            frames == 1
+            and n & (n - 1) == 0
+            and cores == 2
+            and xs == 2
+            and n % cores == 0
+            and width * cores % (n * HEAD) == 0
+            and length % (xs * cores * CHUNKS * 16) == 0
+        )
+        step = functools.partial(spread, n, cores) if fits else gathered
+        return step(queries, keys, values, band_table, windows, out_weight)
+
     return jax.shard_map(
         local,
         mesh=mesh,

time: 171 us -> 65.5 us (0.38)
  waiting for transfers between devices: 105 us -> 14.7 us
  starting transfers between devices: 0.08 us -> 35.9 us
  loops' own time: 16.9 us -> 0 us
  local copies, waits for them, and re-layouts: 18.4 us -> 4.34 us
  between operations: 13.2 us -> 0.21 us
  matrix products: 12.8 us -> 0 us
  Pallas kernels: 0 us -> 10.1 us
  other arithmetic: 4.12 us -> 0.01 us
    all_gather x2 -> x0, waiting for transfers between devices: 76.1 us -> none  [the longest x1 38.6 us: local(): key_part = lax.all_gather(keys, 'tm', axis=0, tiled=True)]
    ppermute x0 -> x21, starting transfers between devices: none -> 35.9 us  [the longest x7 12 us: swapped(): return lax.ppermute(x, axis, [(0, 1), (1, 0)])]
    reduce_scatter x1 -> x0, waiting for transfers between devices: 27.2 us -> none  [local(): lax.psum_scatter(jnp.dot(attended, out_weight, preferred_element_type=jnp...]
    another operation x1 -> x0, loops' own time: 16.9 us -> none  [local(): lax.scan(advance, state, (key_part, value_part, lax.iota(jnp.int32, key_p...]
    dynamic_slice x24 -> x0, local copies, waits for them, and re-layouts: 16.3 us -> none  [the longest x16 8.4 us: local(): lax.scan(advance, state, (key_part, value_part, lax.iota(jnp.int32, key_p...]
    ppermute x0 -> x21, waiting for transfers between devices: none -> 14.7 us  [the longest x4 8.85 us: spread(): own = [lax.ppermute(packed[r], ('tm', 'sub'), rounds[r]) for r in range(n)]]
    dot_general x9 -> x0, matrix products: 12.8 us -> none  [the longest x4 5.8 us: absorb(): jnp.einsum('phd,qhd->hpq', query, key_frame.reshape(length, heads, HEAD),...]
    pallas_call x0 -> x7, Pallas kernels: none -> 10.1 us  [the longest x2 4.31 us: spread(): pl.pallas_call(functools.partial(project_kernel, n, cores), out_shape=[ja...]
  transfers between devices with their start and end apart: 3 -> 21, of which waited for: 3 -> 7; matrix products, arithmetic and copies ran while one was open for 1% -> 0% of each run, Pallas kernels for 0% -> 14%
where the time goes in v1:
time: 65.5 us; the launch traced here: 65.2 us
  starting transfers between devices  35.9 us (55%)
  waiting for transfers between devices  14.7 us (22%)
  Pallas kernels  10.1 us (15%)
  local copies, waits for them, and re-layouts  4.34 us (7%)
    ppermute x7, starting transfers between devices, swapped(): return lax.ppermute(x, axis, [(0, 1), (1, 0)])  12 us
    ppermute x4, starting transfers between devices, spread(): own = [lax.ppermute(packed[r], ('tm', 'sub'), rounds[r]) for r in range(n)]  9.28 us
    ppermute x4, waiting for transfers between devices, spread(): own = [lax.ppermute(packed[r], ('tm', 'sub'), rounds[r]) for r in range(n)]  8.85 us
    ppermute x6, starting transfers between devices, spread(): lax.ppermute(outs[k], 'tm', [(z, z ^ k) for z in range(n)])  8.67 us
    ppermute x4, starting transfers between devices, spread(): query.append(lax.ppermute(block, ('tm', 'sub'), rounds[r]))  5.86 us
    ppermute x7, waiting for transfers between devices, swapped(): return lax.ppermute(x, axis, [(0, 1), (1, 0)])  5.51 us
    unnamed x14, local copies, waits for them, and re-layouts  4.34 us
    pallas_call x2, Pallas kernels, spread(): pl.pallas_call(functools.partial(project_kernel, n, cores), out_shape=[ja...  4.31 us
  transfers between devices with their start and end apart: 21, of which 7 were waited for; matrix products, arithmetic and copies ran while one was open for 0% of the time, Pallas kernels for 14%

profile of v1, /device:TPU:0, one launch (start us, length us, event | category | flops | bytes accessed | tf_op | source)
XLA Modules:
  0.0 65.2 jit_solution(6773695868682252073)
XLA Ops:
  0.0 0.0 copy-start
  0.0 1.0 %copy-done = bf16[1,256,768]{2,1,0:T(8,128)(2,1)S(1)} copy-done((bf16[1,256,768]{2,1,0:T(8,128)(2,1)S(1)}, bf16[1,256,768]{2,1,0:T(8,128)(2,1)}, u32[]{:S(2)}) %copy-start) | copy-done | bytes 393240
  1.0 0.0 copy-start.1
  1.0 1.0 %copy-done.1 = bf16[1,256,768]{2,1,0:T(8,128)(2,1)S(1)} copy-done((bf16[1,256,768]{2,1,0:T(8,128)(2,1)S(1)}, bf16[1,256,768]{2,1,0:T(8,128)(2,1)}, u32[]{:S(2)}) %copy-start.1) | copy-done | bytes 393240
  2.0 0.0 copy-start.2
  2.0 1.0 %copy-done.2 = bf16[1,256,768]{2,1,0:T(8,128)(2,1)S(1)} copy-done((bf16[1,256,768]{2,1,0:T(8,128)(2,1)S(1)}, bf16[1,256,768]{2,1,0:T(8,128)(2,1)}, u32[]{:S(2)}) %copy-start.2) | copy-done | bytes 393240
  3.0 0.4 pack.1
  3.4 0.5 collective-permute-start
  3.9 6.2 %collective-permute-done.rest_1_ = bf16[2,128,384]{2,1,0:T(8,128)(2,1)S(1)} collective-permute-done((bf16[2,128,384]{2,1,0:T(8,128)(2,1)S(1)}, bf16[2,128,384]{2,1,0:T(8,128)(2,1)S(1)}, u32[]{:S(2)}, u32[]{:S(2)}) %collective-permute-start) | collective-permute-done | bytes 196640 | tf_op jit(solution)/shard_map/ppermute | solution.py:245
  10.1 0.0 collective-permute-start.1
  10.1 3.5 %collective-permute-start.3 = (bf16[2,128,384]{2,1,0:T(8,128)(2,1)S(1)}, bf16[2,128,384]{2,1,0:T(8,128)(2,1)S(1)}, u32[]{:S(2)}, u32[]{:S(2)}) collective-permute-start(bf16[2,128,384]{2,1,0:T(8,128)(2,1)S(1)} %get-tuple-element.33), channel_id=1, source_target_pairs={{0,4},{1,12},{4,5},{5,13},{8,0},{9,8},{12,1},{13,9},{2,6},{3,14},{... | collective-permute-start | bytes 589832 | tf_op jit(solution)/shard_map/ppermute | solution.py:245
  13.6 0.7 %collective-permute-start.2 = (bf16[2,128,384]{2,1,0:T(8,128)(2,1)S(1)}, bf16[2,128,384]{2,1,0:T(8,128)(2,1)S(1)}, u32[]{:S(2)}, u32[]{:S(2)}) collective-permute-start(bf16[2,128,384]{2,1,0:T(8,128)(2,1)S(1)} %get-tuple-element.32._), channel_id=1, source_target_pairs={{0,0},{1,8},{4,1},{5,9},{8,4},{9,12},{12,5},{13,13},{2,2},{3,10},{... | collective-permute-start | bytes 589832 | tf_op jit(solution)/shard_map/ppermute | solution.py:245
  14.3 4.6 %collective-permute-start.4 = (bf16[2,128,384]{2,1,0:T(8,128)(2,1)S(1)}, bf16[2,128,384]{2,1,0:T(8,128)(2,1)S(1)}, u32[]{:S(2)}, u32[]{:S(2)}) collective-permute-start(bf16[2,128,384]{2,1,0:T(8,128)(2,1)S(1)} %get-tuple-element.34), channel_id=1, source_target_pairs={{0,5},{1,13},{4,4},{5,12},{8,1},{9,9},{12,0},{13,8},{2,7},{3,15},{... | collective-permute-start | bytes 589832 | tf_op jit(solution)/shard_map/ppermute | solution.py:245
  18.9 0.1 collective-permute-start.10
  18.9 1.5 %collective-permute-done.3.rest_2_ = bf16[2,128,384]{2,1,0:T(8,128)(2,1)S(1)} collective-permute-done((bf16[2,128,384]{2,1,0:T(8,128)(2,1)S(1)}, bf16[2,128,384]{2,1,0:T(8,128)(2,1)S(1)}, u32[]{:S(2)}, u32[]{:S(2)}) %collective-permute-start.3) | collective-permute-done | bytes 196640 | tf_op jit(solution)/shard_map/ppermute | solution.py:245
  20.5 0.5 collective-permute-start.11
  21.0 0.0 collective-permute-done.2.rest_0_
  21.0 4.5 %collective-permute-start.12 = (bf16[128,384]{1,0:T(8,128)(2,1)S(1)}, bf16[128,384]{1,0:T(8,128)(2,1)S(1)}, u32[]{:S(2)}, u32[]{:S(2)}) collective-permute-start(bf16[128,384]{1,0:T(8,128)(2,1)S(1)} %get-tuple-element.42), channel_id=1, source_target_pairs={{0,5},{1,13},{4,4},{5,12},{8,1},{9,9},{12,0},{13,8},{2,7},{3,15},{... | collective-permute-start | bytes 294920 | tf_op jit(solution)/shard_map/ppermute | solution.py:249
  25.5 0.0 slice-start
  25.5 1.1 %collective-permute-done.4.rest_3_ = bf16[2,128,384]{2,1,0:T(8,128)(2,1)S(1)} collective-permute-done((bf16[2,128,384]{2,1,0:T(8,128)(2,1)S(1)}, bf16[2,128,384]{2,1,0:T(8,128)(2,1)S(1)}, u32[]{:S(2)}, u32[]{:S(2)}) %collective-permute-start.4) | collective-permute-done | bytes 196640 | tf_op jit(solution)/shard_map/ppermute | solution.py:245
  26.6 0.8 %collective-permute-start.9 = (bf16[128,384]{1,0:T(8,128)(2,1)S(1)}, bf16[128,384]{1,0:T(8,128)(2,1)S(1)}, u32[]{:S(2)}, u32[]{:S(2)}) collective-permute-start(bf16[128,384]{1,0:T(8,128)(2,1)S(1)} %get-tuple-element.36), channel_id=1, source_target_pairs={{0,0},{1,8},{4,1},{5,9},{8,4},{9,12},{12,5},{13,13},{2,2},{3,10},{... | collective-permute-start | bytes 294920 | tf_op jit(solution)/shard_map/ppermute | solution.py:249
  27.4 0.0 collective-permute-done.10.rest_9_
  27.4 6.0 %collective-permute-start.6 = (bf16[2,128,384]{2,1,0:T(8,128)(2,1)S(1)}, bf16[2,128,384]{2,1,0:T(8,128)(2,1)S(1)}, u32[]{:S(2)}, u32[]{:S(2)}) collective-permute-start(bf16[2,128,384]{2,1,0:T(8,128)(2,1)S(1)} %collective-permute-done.rest_1_), channel_id=1, source_target_pairs={{0,1},{1,0},{2,3},{3,2},{4,5},{5,4},{6,7},{7,6},{8,9},{9,8},{10,11... | collective-permute-start | bytes 589832 | tf_op jit(solution)/shard_map/ppermute | solution.py:214
  33.4 0.1 collective-permute-done.11.rest_10_
  33.5 0.0 collective-permute-start.7
  33.5 0.0 collective-permute-done.12.rest_11_
  33.5 0.9 %collective-permute-start.8 = (bf16[2,128,384]{2,1,0:T(8,128)(2,1)S(1)}, bf16[2,128,384]{2,1,0:T(8,128)(2,1)S(1)}, u32[]{:S(2)}, u32[]{:S(2)}) collective-permute-start(bf16[2,128,384]{2,1,0:T(8,128)(2,1)S(1)} %collective-permute-done.4.rest_3_), channel_id=1, source_target_pairs={{0,1},{1,0},{2,3},{3,2},{4,5},{5,4},{6,7},{7,6},{8,9},{9,8},{10,11... | collective-permute-start | bytes 589832 | tf_op jit(solution)/shard_map/ppermute | solution.py:214
  34.3 0.0 collective-permute-done.9.rest_8_
  34.4 2.9 %collective-permute-start.5 = (bf16[2,128,384]{2,1,0:T(8,128)(2,1)S(1)}, bf16[2,128,384]{2,1,0:T(8,128)(2,1)S(1)}, u32[]{:S(2)}, u32[]{:S(2)}) collective-permute-start(bf16[2,128,384]{2,1,0:T(8,128)(2,1)S(1)} %collective-permute-done.2.rest_0_), channel_id=1, source_target_pairs={{0,1},{1,0},{2,3},{3,2},{4,5},{5,4},{6,7},{7,6},{8,9},{9,8},{10,11... | collective-permute-start | bytes 589832 | tf_op jit(solution)/shard_map/ppermute | solution.py:214
  37.3 0.0 copy-start.3
  37.3 0.7 %copy-done.3 = s32[4,4]{1,0:T(4,128)S(1)} copy-done((s32[4,4]{1,0:T(4,128)S(1)}, s32[4,4]{1,0:T(4,128)}, u32[]{:S(2)}) %copy-start.3) | copy-done | bytes 88
  38.0 0.0 copy-start.4
  38.0 0.7 %copy-done.4 = s32[7]{0:T(128)S(1)} copy-done((s32[7]{0:T(128)S(1)}, s32[7]{0:T(128)}, u32[]{:S(2)}) %copy-start.4) | copy-done | bytes 52
  38.6 0.7 %bias.1.bias_ref = f32[512,1024]{1,0:T(8,128)S(1)} custom-call(s32[4,4]{1,0:T(4,128)S(1)} %copy-done.3, s32[7]{0:T(128)S(1)} %copy-done.4, bf16[2,128,384]{2,1,0:T(8,128)(2,1)S(1)} %get-tuple-element.32._), custom_call_target="tpu_custom_call" | custom-call | tf_op jit(solution)/shard_map/bias/pallas_call | solution.py:254
  39.4 0.0 slice-start.1
  39.4 0.0 collective-permute-done.6.rest_5_
  39.4 0.0 collective-permute-done.7.rest_6_
  39.4 0.0 collective-permute-done.8.rest_7_
  39.4 0.0 collective-permute-done.5.rest_4_
  39.4 1.9 %attend.3 = (bf16[64,384]{1,0:T(8,128)(2,1)S(1)}, bf16[64,384]{1,0:T(8,128)(2,1)S(1)}, bf16[64,384]{1,0:T(8,128)(2,1)S(1)}, bf16[64,384]{1,0:T(8,128)(2,1)S(1)}) custom-call(f32[512,1024]{1,0:T(8,128)S(1)} %bias.1.bias_ref, bf16[2,128,384]{2,1,0:T(8,128)(2,1)S(1)} %collective-permute-done.2.rest_0_, bf16[2,128,384]{2,1,0:T(8,128)(2,1)S(1)} %collective-permute-done.rest_1_, ...), custom_call_target="tpu_custom_call" | custom-call | tf_op jit(solution)/shard_map/attend/pallas_call | solution.py:267
  41.4 0.1 collective-permute-start.17
  41.4 0.9 %collective-permute-start.18 = (bf16[64,384]{1,0:T(8,128)(2,1)S(1)}, bf16[64,384]{1,0:T(8,128)(2,1)S(1)}, u32[]{:S(2)}, u32[]{:S(2)}) collective-permute-start(bf16[64,384]{1,0:T(8,128)(2,1)S(1)} %get-tuple-element.51), channel_id=1, source_target_pairs={{0,8},{4,12},{8,0},{12,4},{1,9},{5,13},{9,1},{13,5},{2,10},{6,14},... | collective-permute-start | bytes 147464 | tf_op jit(solution)/shard_map/ppermute | solution.py:283
  42.3 3.5 %collective-permute-start.19 = (bf16[64,384]{1,0:T(8,128)(2,1)S(1)}, bf16[64,384]{1,0:T(8,128)(2,1)S(1)}, u32[]{:S(2)}, u32[]{:S(2)}) collective-permute-start(bf16[64,384]{1,0:T(8,128)(2,1)S(1)} %get-tuple-element.52), channel_id=1, source_target_pairs={{0,12},{4,8},{8,4},{12,0},{1,13},{5,9},{9,5},{13,1},{2,14},{6,10},... | collective-permute-start | bytes 147464 | tf_op jit(solution)/shard_map/ppermute | solution.py:283
  45.8 1.9 %attend.2 = (bf16[64,384]{1,0:T(8,128)(2,1)S(1)}, bf16[64,384]{1,0:T(8,128)(2,1)S(1)}, bf16[64,384]{1,0:T(8,128)(2,1)S(1)}, bf16[64,384]{1,0:T(8,128)(2,1)S(1)}) custom-call(f32[512,1024]{1,0:T(8,128)S(1)} %bias.1.bias_ref, bf16[2,128,384]{2,1,0:T(8,128)(2,1)S(1)} %collective-permute-done.2.rest_0_, bf16[2,128,384]{2,1,0:T(8,128)(2,1)S(1)} %collective-permute-done.rest_1_, ...), custom_call_target="tpu_custom_call" | custom-call | tf_op jit(solution)/shard_map/attend/pallas_call | solution.py:267
  47.7 0.1 collective-permute-start.13
  47.8 0.0 collective-permute-done.17.rest_1_
  47.8 0.9 %collective-permute-start.14 = (bf16[64,384]{1,0:T(8,128)(2,1)S(1)}, bf16[64,384]{1,0:T(8,128)(2,1)S(1)}, u32[]{:S(2)}, u32[]{:S(2)}) collective-permute-start(bf16[64,384]{1,0:T(8,128)(2,1)S(1)} %get-tuple-element.45), channel_id=1, source_target_pairs={{0,8},{4,12},{8,0},{12,4},{1,9},{5,13},{9,1},{13,5},{2,10},{6,14},... | collective-permute-start | bytes 147464 | tf_op jit(solution)/shard_map/ppermute | solution.py:283
  48.7 0.2 collective-permute-done.18.rest_2_
  48.9 3.3 %collective-permute-start.15 = (bf16[64,384]{1,0:T(8,128)(2,1)S(1)}, bf16[64,384]{1,0:T(8,128)(2,1)S(1)}, u32[]{:S(2)}, u32[]{:S(2)}) collective-permute-start(bf16[64,384]{1,0:T(8,128)(2,1)S(1)} %get-tuple-element.46), channel_id=1, source_target_pairs={{0,12},{4,8},{8,4},{12,0},{1,13},{5,9},{9,5},{13,1},{2,14},{6,10},... | collective-permute-start | bytes 147464 | tf_op jit(solution)/shard_map/ppermute | solution.py:283
  52.2 0.0 collective-permute-done.19.rest_3_
  52.2 0.0 collective-permute-done.1.other_w
  52.2 0.0 slice-done
  52.2 0.0 slice-done.1
  52.2 2.2 %project.3 = (f32[32,3072]{1,0:T(8,128)S(1)}, bf16[32,3072]{1,0:T(8,128)(2,1)S(1)}) custom-call(bf16[768,3072]{1,0:T(8,128)(2,1)S(1)} %bitcast.1, bf16[768,3072]{1,0:T(8,128)(2,1)S(1)} %collective-permute-done.1.other_w, bf16[64,384]{1,0:T(8,128)(2,1)S(1)} %get-tuple-element.49.rest_0_, bf16[64,384]{1,0:T(8,128)(2,1)S(1)} %collective-permute-done.17.rest_1_, ...), custom_call_target="tpu_custom_call" | custom-call | tf_op jit(solution)/shard_map/project/pallas_call | solution.py:285
  54.4 1.7 %collective-permute-start.20 = (bf16[32,3072]{1,0:T(8,128)(2,1)S(1)}, bf16[32,3072]{1,0:T(8,128)(2,1)S(1)}, u32[]{:S(2)}, u32[]{:S(2)}) collective-permute-start(bf16[32,3072]{1,0:T(8,128)(2,1)S(1)} %get-tuple-element.54), channel_id=1, source_target_pairs={{0,2},{2,0},{1,3},{3,1},{4,6},{6,4},{5,7},{7,5},{8,10},{10,8},{9,1... | collective-permute-start | bytes 589832 | tf_op jit(solution)/shard_map/ppermute | solution.py:214
  56.1 0.0 collective-permute-done.13.rest_1_
  56.1 0.0 collective-permute-done.14.rest_2_
  56.1 0.0 collective-permute-done.15.rest_3_
  56.2 2.2 %project.2 = (f32[32,3072]{1,0:T(8,128)S(1)}, bf16[32,3072]{1,0:T(8,128)(2,1)S(1)}) custom-call(bf16[768,3072]{1,0:T(8,128)(2,1)S(1)} %bitcast.1, bf16[768,3072]{1,0:T(8,128)(2,1)S(1)} %collective-permute-done.1.other_w, bf16[64,384]{1,0:T(8,128)(2,1)S(1)} %get-tuple-element.43.rest_0_, bf16[64,384]{1,0:T(8,128)(2,1)S(1)} %collective-permute-done.13.rest_1_, ...), custom_call_target="tpu_custom_call" | custom-call | tf_op jit(solution)/shard_map/project/pallas_call | solution.py:285
  58.3 0.5 collective-permute-start.16
  58.8 2.4 %collective-permute-done.20.refs_3_ = bf16[32,3072]{1,0:T(8,128)(2,1)S(1)} collective-permute-done((bf16[32,3072]{1,0:T(8,128)(2,1)S(1)}, bf16[32,3072]{1,0:T(8,128)(2,1)S(1)}, u32[]{:S(2)}, u32[]{:S(2)}) %collective-permute-start.20) | collective-permute-done | bytes 196640 | tf_op jit(solution)/shard_map/ppermute | solution.py:214
  61.2 3.1 %collective-permute-done.16.refs_1_ = bf16[32,3072]{1,0:T(8,128)(2,1)S(1)} collective-permute-done((bf16[32,3072]{1,0:T(8,128)(2,1)S(1)}, bf16[32,3072]{1,0:T(8,128)(2,1)S(1)}, u32[]{:S(2)}, u32[]{:S(2)}) %collective-permute-start.16) | collective-permute-done | bytes 196640 | tf_op jit(solution)/shard_map/ppermute | solution.py:214
  64.3 0.8 %add.1 = bf16[1,64,3072]{2,1,0:T(8,128)(2,1)} custom-call(f32[32,3072]{1,0:T(8,128)S(1)} %get-tuple-element.47.refs_0_, bf16[32,3072]{1,0:T(8,128)(2,1)S(1)} %collective-permute-done.16.refs_1_, f32[32,3072]{1,0:T(8,128)S(1)} %get-tuple-element.53.refs_2_, bf16[32,3072]{1,0:T(8,128)(2,1)S(1)} %collective-permute-done.20.refs_3_), custom_call_target="tpu_custom_call" | custom-call | tf_op jit(solution)/shard_map/add/pallas_call | solution.py:301
  (1 shorter events, 0.0 us)
Async XLA Ops:
  0.0 1.0 %copy-start = (bf16[1,256,768]{2,1,0:T(8,128)(2,1)S(1)}, bf16[1,256,768]{2,1,0:T(8,128)(2,1)}, u32[]{:S(2)}) copy-start(bf16[1,256,768]{2,1,0:T(8,128)(2,1)} %q_ref.1) | copy-start | bytes 1179652
  1.0 1.0 %copy-start.1 = (bf16[1,256,768]{2,1,0:T(8,128)(2,1)S(1)}, bf16[1,256,768]{2,1,0:T(8,128)(2,1)}, u32[]{:S(2)}) copy-start(bf16[1,256,768]{2,1,0:T(8,128)(2,1)} %k_ref.1) | copy-start | bytes 1179652
  2.0 1.0 %copy-start.2 = (bf16[1,256,768]{2,1,0:T(8,128)(2,1)S(1)}, bf16[1,256,768]{2,1,0:T(8,128)(2,1)}, u32[]{:S(2)}) copy-start(bf16[1,256,768]{2,1,0:T(8,128)(2,1)} %v_ref.1) | copy-start | bytes 1179652
  3.4 6.7 %collective-permute-start = (bf16[2,128,384]{2,1,0:T(8,128)(2,1)S(1)}, bf16[2,128,384]{2,1,0:T(8,128)(2,1)S(1)}, u32[]{:S(2)}, u32[]{:S(2)}) collective-permute-start(bf16[2,128,384]{2,1,0:T(8,128)(2,1)S(1)} %get-tuple-element.30), channel_id=1, source_target_pairs={{0,1},{1,9},{4,0},{5,8},{8,5},{9,13},{12,4},{13,12},{2,3},{3,11},{... | collective-permute-start | bytes 589832 | tf_op jit(solution)/shard_map/ppermute | solution.py:245
  10.1 42.1 %collective-permute-start.1 = (bf16[768,3072]{1,0:T(8,128)(2,1)}, bf16[768,3072]{1,0:T(8,128)(2,1)S(1)}, u32[]{:S(2)}, u32[]{:S(2)}) collective-permute-start(bf16[768,3072]{1,0:T(8,128)(2,1)} %own_w.3), channel_id=1, source_target_pairs={{0,1},{1,0},{2,3},{3,2},{4,5},{5,4},{6,7},{7,6},{8,9},{9,8},{10,11... | collective-permute-start | bytes 14155784 | tf_op jit(solution)/shard_map/ppermute | solution.py:214
  10.1 10.4 %collective-permute-start.3 = (bf16[2,128,384]{2,1,0:T(8,128)(2,1)S(1)}, bf16[2,128,384]{2,1,0:T(8,128)(2,1)S(1)}, u32[]{:S(2)}, u32[]{:S(2)}) collective-permute-start(bf16[2,128,384]{2,1,0:T(8,128)(2,1)S(1)} %get-tuple-element.33), channel_id=1, source_target_pairs={{0,4},{1,12},{4,5},{5,13},{8,0},{9,8},{12,1},{13,9},{2,6},{3,14},{... | collective-permute-start | bytes 589832 | tf_op jit(solution)/shard_map/ppermute | solution.py:245
  13.6 7.4 %collective-permute-start.2 = (bf16[2,128,384]{2,1,0:T(8,128)(2,1)S(1)}, bf16[2,128,384]{2,1,0:T(8,128)(2,1)S(1)}, u32[]{:S(2)}, u32[]{:S(2)}) collective-permute-start(bf16[2,128,384]{2,1,0:T(8,128)(2,1)S(1)} %get-tuple-element.32._), channel_id=1, source_target_pairs={{0,0},{1,8},{4,1},{5,9},{8,4},{9,12},{12,5},{13,13},{2,2},{3,10},{... | collective-permute-start | bytes 589832 | tf_op jit(solution)/shard_map/ppermute | solution.py:245
  14.3 12.3 %collective-permute-start.4 = (bf16[2,128,384]{2,1,0:T(8,128)(2,1)S(1)}, bf16[2,128,384]{2,1,0:T(8,128)(2,1)S(1)}, u32[]{:S(2)}, u32[]{:S(2)}) collective-permute-start(bf16[2,128,384]{2,1,0:T(8,128)(2,1)S(1)} %get-tuple-element.34), channel_id=1, source_target_pairs={{0,5},{1,13},{4,4},{5,12},{8,1},{9,9},{12,0},{13,8},{2,7},{3,15},{... | collective-permute-start | bytes 589832 | tf_op jit(solution)/shard_map/ppermute | solution.py:245
  18.9 8.5 %collective-permute-start.10 = (bf16[128,384]{1,0:T(8,128)(2,1)S(1)}, bf16[128,384]{1,0:T(8,128)(2,1)S(1)}, u32[]{:S(2)}, u32[]{:S(2)}) collective-permute-start(bf16[128,384]{1,0:T(8,128)(2,1)S(1)} %get-tuple-element.38), channel_id=1, source_target_pairs={{0,1},{1,9},{4,0},{5,8},{8,5},{9,13},{12,4},{13,12},{2,3},{3,11},{... | collective-permute-start | bytes 294920 | tf_op jit(solution)/shard_map/ppermute | solution.py:249
  20.5 13.0 %collective-permute-start.11 = (bf16[128,384]{1,0:T(8,128)(2,1)S(1)}, bf16[128,384]{1,0:T(8,128)(2,1)S(1)}, u32[]{:S(2)}, u32[]{:S(2)}) collective-permute-start(bf16[128,384]{1,0:T(8,128)(2,1)S(1)} %get-tuple-element.40), channel_id=1, source_target_pairs={{0,4},{1,12},{4,5},{5,13},{8,0},{9,8},{12,1},{13,9},{2,6},{3,14},{... | collective-permute-start | bytes 294920 | tf_op jit(solution)/shard_map/ppermute | solution.py:249
  21.0 12.5 %collective-permute-start.12 = (bf16[128,384]{1,0:T(8,128)(2,1)S(1)}, bf16[128,384]{1,0:T(8,128)(2,1)S(1)}, u32[]{:S(2)}, u32[]{:S(2)}) collective-permute-start(bf16[128,384]{1,0:T(8,128)(2,1)S(1)} %get-tuple-element.42), channel_id=1, source_target_pairs={{0,5},{1,13},{4,4},{5,12},{8,1},{9,9},{12,0},{13,8},{2,7},{3,15},{... | collective-permute-start | bytes 294920 | tf_op jit(solution)/shard_map/ppermute | solution.py:249
  25.5 26.7 %slice-start = ((s8[4718592]{0:T(1024)(128)(4,1)}), s8[4194304]{0:T(1024)(128)(4,1)S(1)}, s32[]{:S(2)}) async-start(s8[4718592]{0:T(1024)(128)(4,1)} %bitcast), calls=%async_computation | async-start | bytes 8388608
  26.6 7.7 %collective-permute-start.9 = (bf16[128,384]{1,0:T(8,128)(2,1)S(1)}, bf16[128,384]{1,0:T(8,128)(2,1)S(1)}, u32[]{:S(2)}, u32[]{:S(2)}) collective-permute-start(bf16[128,384]{1,0:T(8,128)(2,1)S(1)} %get-tuple-element.36), channel_id=1, source_target_pairs={{0,0},{1,8},{4,1},{5,9},{8,4},{9,12},{12,5},{13,13},{2,2},{3,10},{... | collective-permute-start | bytes 294920 | tf_op jit(solution)/shard_map/ppermute | solution.py:249
  27.4 12.0 %collective-permute-start.6 = (bf16[2,128,384]{2,1,0:T(8,128)(2,1)S(1)}, bf16[2,128,384]{2,1,0:T(8,128)(2,1)S(1)}, u32[]{:S(2)}, u32[]{:S(2)}) collective-permute-start(bf16[2,128,384]{2,1,0:T(8,128)(2,1)S(1)} %collective-permute-done.rest_1_), channel_id=1, source_target_pairs={{0,1},{1,0},{2,3},{3,2},{4,5},{5,4},{6,7},{7,6},{8,9},{9,8},{10,11... | collective-permute-start | bytes 589832 | tf_op jit(solution)/shard_map/ppermute | solution.py:214
  33.5 5.9 %collective-permute-start.7 = (bf16[2,128,384]{2,1,0:T(8,128)(2,1)S(1)}, bf16[2,128,384]{2,1,0:T(8,128)(2,1)S(1)}, u32[]{:S(2)}, u32[]{:S(2)}) collective-permute-start(bf16[2,128,384]{2,1,0:T(8,128)(2,1)S(1)} %collective-permute-done.3.rest_2_), channel_id=1, source_target_pairs={{0,1},{1,0},{2,3},{3,2},{4,5},{5,4},{6,7},{7,6},{8,9},{9,8},{10,11... | collective-permute-start | bytes 589832 | tf_op jit(solution)/shard_map/ppermute | solution.py:214
  33.5 5.9 %collective-permute-start.8 = (bf16[2,128,384]{2,1,0:T(8,128)(2,1)S(1)}, bf16[2,128,384]{2,1,0:T(8,128)(2,1)S(1)}, u32[]{:S(2)}, u32[]{:S(2)}) collective-permute-start(bf16[2,128,384]{2,1,0:T(8,128)(2,1)S(1)} %collective-permute-done.4.rest_3_), channel_id=1, source_target_pairs={{0,1},{1,0},{2,3},{3,2},{4,5},{5,4},{6,7},{7,6},{8,9},{9,8},{10,11... | collective-permute-start | bytes 589832 | tf_op jit(solution)/shard_map/ppermute | solution.py:214
  34.4 5.1 %collective-permute-start.5 = (bf16[2,128,384]{2,1,0:T(8,128)(2,1)S(1)}, bf16[2,128,384]{2,1,0:T(8,128)(2,1)S(1)}, u32[]{:S(2)}, u32[]{:S(2)}) collective-permute-start(bf16[2,128,384]{2,1,0:T(8,128)(2,1)S(1)} %collective-permute-done.2.rest_0_), channel_id=1, source_target_pairs={{0,1},{1,0},{2,3},{3,2},{4,5},{5,4},{6,7},{7,6},{8,9},{9,8},{10,11... | collective-permute-start | bytes 589832 | tf_op jit(solution)/shard_map/ppermute | solution.py:214
  37.3 0.7 %copy-start.3 = (s32[4,4]{1,0:T(4,128)S(1)}, s32[4,4]{1,0:T(4,128)}, u32[]{:S(2)}) copy-start(s32[4,4]{1,0:T(4,128)} %band_ref.1) | copy-start | bytes 196
  38.0 0.7 %copy-start.4 = (s32[7]{0:T(128)S(1)}, s32[7]{0:T(128)}, u32[]{:S(2)}) copy-start(s32[7]{0:T(128)} %reach_ref.1) | copy-start | bytes 88
  39.4 12.8 %slice-start.1 = ((s8[4718592]{0:T(1024)(128)(4,1)}), s8[524288]{0:T(1024)(128)(4,1)S(1)}, s32[]{:S(2)}) async-start(s8[4718592]{0:T(1024)(128)(4,1)} %bitcast), calls=%async_computation.1 | async-start | bytes 1048576
  41.4 6.5 %collective-permute-start.17 = (bf16[64,384]{1,0:T(8,128)(2,1)S(1)}, bf16[64,384]{1,0:T(8,128)(2,1)S(1)}, u32[]{:S(2)}, u32[]{:S(2)}) collective-permute-start(bf16[64,384]{1,0:T(8,128)(2,1)S(1)} %get-tuple-element.50), channel_id=1, source_target_pairs={{0,4},{4,0},{8,12},{12,8},{1,5},{5,1},{9,13},{13,9},{2,6},{6,2},{1... | collective-permute-start | bytes 147464 | tf_op jit(solution)/shard_map/ppermute | solution.py:283
  41.4 7.5 %collective-permute-start.18 = (bf16[64,384]{1,0:T(8,128)(2,1)S(1)}, bf16[64,384]{1,0:T(8,128)(2,1)S(1)}, u32[]{:S(2)}, u32[]{:S(2)}) collective-permute-start(bf16[64,384]{1,0:T(8,128)(2,1)S(1)} %get-tuple-element.51), channel_id=1, source_target_pairs={{0,8},{4,12},{8,0},{12,4},{1,9},{5,13},{9,1},{13,5},{2,10},{6,14},... | collective-permute-start | bytes 147464 | tf_op jit(solution)/shard_map/ppermute | solution.py:283
  42.3 9.9 %collective-permute-start.19 = (bf16[64,384]{1,0:T(8,128)(2,1)S(1)}, bf16[64,384]{1,0:T(8,128)(2,1)S(1)}, u32[]{:S(2)}, u32[]{:S(2)}) collective-permute-start(bf16[64,384]{1,0:T(8,128)(2,1)S(1)} %get-tuple-element.52), channel_id=1, source_target_pairs={{0,12},{4,8},{8,4},{12,0},{1,13},{5,9},{9,5},{13,1},{2,14},{6,10},... | collective-permute-start | bytes 147464 | tf_op jit(solution)/shard_map/ppermute | solution.py:283
  47.7 8.4 %collective-permute-start.13 = (bf16[64,384]{1,0:T(8,128)(2,1)S(1)}, bf16[64,384]{1,0:T(8,128)(2,1)S(1)}, u32[]{:S(2)}, u32[]{:S(2)}) collective-permute-start(bf16[64,384]{1,0:T(8,128)(2,1)S(1)} %get-tuple-element.44), channel_id=1, source_target_pairs={{0,4},{4,0},{8,12},{12,8},{1,5},{5,1},{9,13},{13,9},{2,6},{6,2},{1... | collective-permute-start | bytes 147464 | tf_op jit(solution)/shard_map/ppermute | solution.py:283
  47.8 8.3 %collective-permute-start.14 = (bf16[64,384]{1,0:T(8,128)(2,1)S(1)}, bf16[64,384]{1,0:T(8,128)(2,1)S(1)}, u32[]{:S(2)}, u32[]{:S(2)}) collective-permute-start(bf16[64,384]{1,0:T(8,128)(2,1)S(1)} %get-tuple-element.45), channel_id=1, source_target_pairs={{0,8},{4,12},{8,0},{12,4},{1,9},{5,13},{9,1},{13,5},{2,10},{6,14},... | collective-permute-start | bytes 147464 | tf_op jit(solution)/shard_map/ppermute | solution.py:283
  48.9 7.3 %collective-permute-start.15 = (bf16[64,384]{1,0:T(8,128)(2,1)S(1)}, bf16[64,384]{1,0:T(8,128)(2,1)S(1)}, u32[]{:S(2)}, u32[]{:S(2)}) collective-permute-start(bf16[64,384]{1,0:T(8,128)(2,1)S(1)} %get-tuple-element.46), channel_id=1, source_target_pairs={{0,12},{4,8},{8,4},{12,0},{1,13},{5,9},{9,5},{13,1},{2,14},{6,10},... | collective-permute-start | bytes 147464 | tf_op jit(solution)/shard_map/ppermute | solution.py:283
  54.4 6.8 %collective-permute-start.20 = (bf16[32,3072]{1,0:T(8,128)(2,1)S(1)}, bf16[32,3072]{1,0:T(8,128)(2,1)S(1)}, u32[]{:S(2)}, u32[]{:S(2)}) collective-permute-start(bf16[32,3072]{1,0:T(8,128)(2,1)S(1)} %get-tuple-element.54), channel_id=1, source_target_pairs={{0,2},{2,0},{1,3},{3,1},{4,6},{6,4},{5,7},{7,5},{8,10},{10,8},{9,1... | collective-permute-start | bytes 589832 | tf_op jit(solution)/shard_map/ppermute | solution.py:214
  58.3 6.0 %collective-permute-start.16 = (bf16[32,3072]{1,0:T(8,128)(2,1)S(1)}, bf16[32,3072]{1,0:T(8,128)(2,1)S(1)}, u32[]{:S(2)}, u32[]{:S(2)}) collective-permute-start(bf16[32,3072]{1,0:T(8,128)(2,1)S(1)} %get-tuple-element.48), channel_id=1, source_target_pairs={{0,2},{2,0},{1,3},{3,1},{4,6},{6,4},{5,7},{7,5},{8,10},{10,8},{9,1... | collective-permute-start | bytes 589832 | tf_op jit(solution)/shard_map/ppermute | solution.py:214

commit v2 on v1

--- a/solution.py
+++ b/solution.py
@@ -10,8 +10,12 @@
 HEAD = 128
 ANY = pl.BlockSpec(memory_space=pl.ANY)
 VMEM = pl.BlockSpec(memory_space=pltpu.VMEM)
+HBM = pl.BlockSpec(memory_space=pltpu.HBM)
 SMEM = pl.BlockSpec(memory_space=pltpu.SMEM)
 CHUNKS = 2
+PACK_MB = 59
+TIE = 0
+PIECES = 1
 
 
 def gathered(queries, keys, values, band_table, windows, out_weight):
@@ -86,25 +90,31 @@
 
 
 def pack_kernel(n, cores, tokens, q_ref, k_ref, v_ref, *rest):
-    kv_out, q_out, sem = rest[:n], rest[n : 2 * n], rest[2 * n]
+    outs, held, sem = rest[:n], rest[n], rest[n + 1]
     z = lax.axis_index("tm")
-    wide = kv_out[0].shape[2]
-    half = kv_out[0].shape[1]
-    copies = []
+    _, half, wide = outs[0].shape
+    piece = held.shape[1] // PIECES
+    run_copies(
+        [
+            (ref.at[0, pl.ds(p * piece, piece)], held.at[i, pl.ds(p * piece, piece)])
+            for i, ref in enumerate((k_ref, v_ref, q_ref))
+            for p in range(PIECES)
+        ],
+        sem,
+    )
     for r in range(n):
         t = z ^ r
         cols = pl.ds(pl.multiple_of((t // cores) * wide, wide), wide)
         b = t % cores
         rows = pl.ds(pl.multiple_of(b * half, half), half)
-        copies.append((k_ref.at[0, rows, cols], kv_out[r].at[0]))
-        copies.append((v_ref.at[0, rows, cols], kv_out[r].at[1]))
+        outs[r][0] = held[0, rows, cols]
+        outs[r][1] = held[1, rows, cols]
         for x in range(half // tokens):
             place = pl.ds(pl.multiple_of((x * cores + b) * tokens, tokens), tokens)
-            copies.append((q_ref.at[0, place, cols], q_out[r].at[pl.ds(x * tokens, tokens)]))
-    run_copies(copies, sem)
-
-
-def bias_kernel(n, cores, tokens, band_ref, reach_ref, _, bias_ref):
+            outs[r][2, x * tokens : (x + 1) * tokens] = held[2, place, cols]
+
+
+def bias_kernel(n, cores, tokens, band_ref, reach_ref, bias_ref):
     z, c = lax.axis_index("tm"), lax.axis_index("sub")
     length = bias_ref.shape[1] // n
     half = length // cores
@@ -123,9 +133,8 @@
 
 
 def attend_kernel(n, cores, tokens, first, count, bias_ref, *rest):
-    own, other, query = rest[:n], rest[n : 2 * n], rest[2 * n : 3 * n]
-    outs = rest[3 * n : 4 * n]
-    s_all, p_all, t_all, o_all, sem = rest[4 * n :]
+    own, other, outs = rest[:n], rest[n : 2 * n], rest[2 * n : 3 * n]
+    s_all, p_all, t_all, o_all = rest[3 * n :]
     z, c = lax.axis_index("tm"), lax.axis_index("sub")
     half = own[0].shape[1]
     heads = own[0].shape[2] // HEAD
@@ -141,7 +150,7 @@
         cols = slice(h * HEAD, (h + 1) * HEAD)
         slot = h % 2
         q = jnp.concatenate(
-            [query[r][x * tokens + first : x * tokens + first + count, cols] for r, x, _ in places]
+            [own[r][2, x * tokens + first : x * tokens + first + count, cols] for r, x, _ in places]
         )
         for s in range(n):
             k = jnp.concatenate([own[s][0, :, cols], other[s ^ 1][0, :, cols]])
@@ -173,20 +182,19 @@
         result = (numer * t_all[slot]).astype(jnp.bfloat16)
         for r in range(n):
             o_all[r, :, cols] = result[r * rows : (r + 1) * rows]
-    run_copies([(o_all.at[t ^ z ^ k], outs[k]) for k in range(n)], sem)
+    for k in range(n):
+        outs[k][...] = o_all[t ^ z ^ k]
 
 
 def project_kernel(n, cores, own_w, other_w, *rest):
     parts = rest[:n]
-    keep_ref, send_ref, a_all, sem = rest[n:]
+    keep_ref, send_ref, a_all = rest[n:]
     z, c, x = lax.axis_index("tm"), lax.axis_index("sub"), lax.axis_index("head")
     count = keep_ref.shape[0]
-    copies = []
     for k in range(n):
         for b in range(2):
             at = pl.ds(pl.multiple_of((b ^ 1 ^ x) * count, count), count)
-            copies.append((parts[k].at[at], a_all.at[z ^ k, pl.ds(b * count, count)]))
-    run_copies(copies, sem)
+            a_all[z ^ k, b * count : (b + 1) * count] = parts[k][at, :]
     per = n // cores
     wide = a_all.shape[2]
     total = 0.0
@@ -220,16 +228,20 @@
     wide = width * cores // n
     half = length // cores
     tokens = half // 2
+    count = tokens // CHUNKS
+    rows = 2 * count
     bf16 = queries.dtype
 
     packed = pl.pallas_call(
         functools.partial(pack_kernel, n, cores, tokens),
-        out_shape=[jax.ShapeDtypeStruct((2, half, wide), bf16)] * n
-        + [jax.ShapeDtypeStruct((half, wide), bf16)] * n,
+        out_shape=[jax.ShapeDtypeStruct((3, half, wide), bf16)] * n,
         in_specs=[ANY] * 3,
-        out_specs=[VMEM] * (2 * n),
-        scratch_shapes=[pltpu.SemaphoreType.DMA((4 * n,))],
-        compiler_params=pltpu.CompilerParams(vmem_limit_bytes=4 * 2**20),
+        out_specs=[VMEM] * n,
+        scratch_shapes=[
+            pltpu.VMEM((3, length, width), bf16),
+            pltpu.SemaphoreType.DMA((3 * PIECES,)),
+        ],
+        compiler_params=pltpu.CompilerParams(vmem_limit_bytes=PACK_MB * 2**20),
         name="pack",
     )(queries, keys, values)
 
@@ -242,43 +254,40 @@
         ]
         for r in range(n)
     ]
-    own = [lax.ppermute(packed[r], ("tm", "sub"), rounds[r]) for r in range(n)]
-    query = []
-    for r in range(n):
-        block, _ = lax.optimization_barrier((packed[n + r], own[(r + 1) // 2]))
-        query.append(lax.ppermute(block, ("tm", "sub"), rounds[r]))
-    other = [swapped(block, "sub") for block in own]
-
-    weight, _ = lax.optimization_barrier((out_weight, own[1]))
-    other_weight = swapped(weight, "sub")
     bias = pl.pallas_call(
         functools.partial(bias_kernel, n, cores, tokens),
         out_shape=jax.ShapeDtypeStruct((n * half, n * length), jnp.float32),
-        in_specs=[SMEM, SMEM, ANY],
+        in_specs=[SMEM, SMEM],
         out_specs=VMEM,
         compiler_params=pltpu.CompilerParams(vmem_limit_bytes=4 * 2**20),
         name="bias",
-    )(band_table, windows, packed[0])
-
-    count = tokens // CHUNKS
-    rows = 2 * count
+    )(band_table, windows)
+    blocks = list(packed)
+    blocks[TIE], _ = lax.optimization_barrier((packed[TIE], bias))
+    own = [lax.ppermute(blocks[r], ("tm", "sub"), rounds[r]) for r in range(n)]
+    weight, _ = lax.optimization_barrier((out_weight, packed[0]))
+    other_weight = swapped(weight, "sub")
+    other = []
+    for r in range(n):
+        other.append(swapped(own[r], "sub"))
+    bias, other_weight = lax.optimization_barrier((bias, other_weight))
+
     sums = []
     for a in range(CHUNKS):
         outs = pl.pallas_call(
             functools.partial(attend_kernel, n, cores, tokens, a * count, count),
             out_shape=[jax.ShapeDtypeStruct((rows, wide), bf16)] * n,
-            in_specs=[VMEM] * (1 + 3 * n),
+            in_specs=[VMEM] * (1 + 2 * n),
             out_specs=[VMEM] * n,
             scratch_shapes=[
                 pltpu.VMEM((2, n * rows, n * length), jnp.float32),
                 pltpu.VMEM((2, n * rows, n * length), bf16),
                 pltpu.VMEM((2, n * rows, HEAD), jnp.float32),
                 pltpu.VMEM((n, rows, wide), bf16),
-                pltpu.SemaphoreType.DMA((n,)),
             ],
             compiler_params=pltpu.CompilerParams(vmem_limit_bytes=24 * 2**20),
             name="attend",
-        )(bias, *own, *other, *query)
+        )(bias, *own, *other)
         parts = [outs[0]] + [
             lax.ppermute(outs[k], "tm", [(z, z ^ k) for z in range(n)]) for k in range(1, n)
         ]
@@ -290,10 +299,7 @@
             ],
             in_specs=[VMEM] * (2 + n),
             out_specs=[VMEM] * 2,
-            scratch_shapes=[
-                pltpu.VMEM((n, rows, wide), bf16),
-                pltpu.SemaphoreType.DMA((2 * n,)),
-            ],
+            scratch_shapes=[pltpu.VMEM((n, rows, wide), bf16)],
             compiler_params=pltpu.CompilerParams(vmem_limit_bytes=24 * 2**20),
             name="project",
         )(out_weight, other_weight, *parts)

time: 65.5 us -> 59.3 us (0.905)
  starting transfers between devices: 35.9 us -> 31.5 us
  local copies, waits for them, and re-layouts: 4.34 us -> 1.34 us
  Pallas kernels: 10.1 us -> 10.8 us
  waiting for transfers between devices: 14.7 us -> 15.4 us
    ppermute x8 -> x4, starting transfers between devices: 15.1 us -> 8.72 us  [spread(): own = [lax.ppermute(blocks[r], ('tm', 'sub'), rounds[r]) for r in range(n)]]
    unnamed x14 -> x8, local copies, waits for them, and re-layouts: 4.34 us -> 1.34 us
    ppermute x6, starting transfers between devices: 8.67 us -> 10.8 us  [spread(): lax.ppermute(outs[k], 'tm', [(z, z ^ k) for z in range(n)])]
    pallas_call x1, Pallas kernels: 0.36 us -> 2.4 us  [spread(): pl.pallas_call(functools.partial(pack_kernel, n, cores, tokens), out_shap...]
    ppermute x7, waiting for transfers between devices: 5.51 us -> 6.47 us  [swapped(): return lax.ppermute(x, axis, [(0, 1), (1, 0)])]
    pallas_call x2, Pallas kernels: 4.31 us -> 3.59 us  [spread(): pl.pallas_call(functools.partial(project_kernel, n, cores), out_shape=[ja...]
    ppermute x8 -> x4, waiting for transfers between devices: 8.96 us -> 8.72 us  [spread(): own = [lax.ppermute(blocks[r], ('tm', 'sub'), rounds[r]) for r in range(n)]]
  transfers between devices with their start and end apart: 21 -> 17, of which waited for: 7 -> 7; matrix products, arithmetic and copies ran while one was open for 0% -> 0% of each run, Pallas kernels for 14% -> 10%
where the time goes in v2:
time: 59.3 us; the launch traced here: 59.1 us
  starting transfers between devices  31.5 us (53%)
  waiting for transfers between devices  15.4 us (26%)
  Pallas kernels  10.8 us (18%)
  local copies, waits for them, and re-layouts  1.34 us (2%)
    ppermute x7, starting transfers between devices, swapped(): return lax.ppermute(x, axis, [(0, 1), (1, 0)])  11.9 us
    ppermute x6, starting transfers between devices, spread(): lax.ppermute(outs[k], 'tm', [(z, z ^ k) for z in range(n)])  10.8 us
    ppermute x4, waiting for transfers between devices, spread(): own = [lax.ppermute(blocks[r], ('tm', 'sub'), rounds[r]) for r in range(n)]  8.72 us
    ppermute x4, starting transfers between devices, spread(): own = [lax.ppermute(blocks[r], ('tm', 'sub'), rounds[r]) for r in range(n)]  8.72 us
    ppermute x7, waiting for transfers between devices, swapped(): return lax.ppermute(x, axis, [(0, 1), (1, 0)])  6.47 us
    pallas_call x2, Pallas kernels, spread(): pl.pallas_call(functools.partial(project_kernel, n, cores), out_shape=[ja...  3.59 us
    pallas_call x2, Pallas kernels, spread(): pl.pallas_call(functools.partial(attend_kernel, n, cores, tokens, a * cou...  3.26 us
    pallas_call x1, Pallas kernels, spread(): pl.pallas_call(functools.partial(pack_kernel, n, cores, tokens), out_shap...  2.4 us
  transfers between devices with their start and end apart: 17, of which 7 were waited for; matrix products, arithmetic and copies ran while one was open for 0% of the time, Pallas kernels for 10%

profile of v2, /device:TPU:0, one launch (start us, length us, event | category | flops | bytes accessed | tf_op | source)
XLA Modules:
  0.0 59.1 jit_solution(4796414258818973020)
XLA Ops:
  0.0 2.4 %pack.1 = (bf16[3,128,384]{2,1,0:T(8,128)(2,1)}, bf16[3,128,384]{2,1,0:T(8,128)(2,1)}, bf16[3,128,384]{2,1,0:T(8,128)(2,1)}, bf16[3,128,384]{2,1,0:T(8,128)(2,1)}) custom-call(bf16[1,256,768]{2,1,0:T(8,128)(2,1)} %q_ref.1, bf16[1,256,768]{2,1,0:T(8,128)(2,1)} %k_ref.1, bf16[1,256,768]{2,1,0:T(8,128)(2,1)} %v_ref.1), custom_call_target="tpu_custom_call" | custom-call | tf_op jit(solution)/shard_map/pack/pallas_call | solution.py:235
  2.4 0.5 collective-permute-start
  2.9 0.1 collective-permute-start.2
  3.0 2.6 %collective-permute-start.3 = (bf16[3,128,384]{2,1,0:T(8,128)(2,1)}, bf16[3,128,384]{2,1,0:T(8,128)(2,1)S(1)}, u32[]{:S(2)}, u32[]{:S(2)}) collective-permute-start(bf16[3,128,384]{2,1,0:T(8,128)(2,1)} %get-tuple-element.31), channel_id=1, source_target_pairs={{0,4},{1,12},{4,5},{5,13},{8,0},{9,8},{12,1},{13,9},{2,6},{3,14},{... | collective-permute-start | bytes 884744 | tf_op jit(solution)/shard_map/ppermute | solution.py:267
  5.6 4.2 %collective-permute-start.4 = (bf16[3,128,384]{2,1,0:T(8,128)(2,1)}, bf16[3,128,384]{2,1,0:T(8,128)(2,1)S(1)}, u32[]{:S(2)}, u32[]{:S(2)}) collective-permute-start(bf16[3,128,384]{2,1,0:T(8,128)(2,1)} %get-tuple-element.32), channel_id=1, source_target_pairs={{0,5},{1,13},{4,4},{5,12},{8,1},{9,9},{12,0},{13,8},{2,7},{3,15},{... | collective-permute-start | bytes 884744 | tf_op jit(solution)/shard_map/ppermute | solution.py:267
  9.9 0.0 copy-start
  9.9 0.7 %copy-done = s32[4,4]{1,0:T(4,128)S(1)} copy-done((s32[4,4]{1,0:T(4,128)S(1)}, s32[4,4]{1,0:T(4,128)}, u32[]{:S(2)}) %copy-start) | copy-done | bytes 88
  10.6 0.0 copy-start.1
  10.6 0.7 %copy-done.1 = s32[7]{0:T(128)S(1)} copy-done((s32[7]{0:T(128)S(1)}, s32[7]{0:T(128)}, u32[]{:S(2)}) %copy-start.1) | copy-done | bytes 52
  11.2 0.0 slice-start
  11.2 0.7 %bias.1.bias_ref = f32[512,1024]{1,0:T(8,128)S(1)} custom-call(s32[4,4]{1,0:T(4,128)S(1)} %copy-done, s32[7]{0:T(128)S(1)} %copy-done.1), custom_call_target="tpu_custom_call" | custom-call | tf_op jit(solution)/shard_map/bias/pallas_call | solution.py:257
  12.0 0.0 slice-start.1
  12.0 1.8 %collective-permute-start.1 = (bf16[3,128,384]{2,1,0:T(8,128)(2,1)}, bf16[3,128,384]{2,1,0:T(8,128)(2,1)S(1)}, u32[]{:S(2)}, u32[]{:S(2)}) collective-permute-start(bf16[3,128,384]{2,1,0:T(8,128)(2,1)} %get-tuple-element.29), channel_id=1, source_target_pairs={{0,0},{1,8},{4,1},{5,9},{8,4},{9,12},{12,5},{13,13},{2,2},{3,10},{... | collective-permute-start | bytes 884744 | tf_op jit(solution)/shard_map/ppermute | solution.py:267
  13.7 0.0 collective-permute-done.2.rest_1_
  13.8 3.1 %collective-permute-start.6 = (bf16[3,128,384]{2,1,0:T(8,128)(2,1)S(1)}, bf16[3,128,384]{2,1,0:T(8,128)(2,1)S(1)}, u32[]{:S(2)}, u32[]{:S(2)}) collective-permute-start(bf16[3,128,384]{2,1,0:T(8,128)(2,1)S(1)} %collective-permute-done.2.rest_1_), channel_id=1, source_target_pairs={{0,1},{1,0},{2,3},{3,2},{4,5},{5,4},{6,7},{7,6},{8,9},{9,8},{10,11... | collective-permute-start | bytes 884744 | tf_op jit(solution)/shard_map/ppermute | solution.py:222
  16.8 4.8 %collective-permute-done.3.rest_2_ = bf16[3,128,384]{2,1,0:T(8,128)(2,1)S(1)} collective-permute-done((bf16[3,128,384]{2,1,0:T(8,128)(2,1)}, bf16[3,128,384]{2,1,0:T(8,128)(2,1)S(1)}, u32[]{:S(2)}, u32[]{:S(2)}) %collective-permute-start.3) | collective-permute-done | bytes 294944 | tf_op jit(solution)/shard_map/ppermute | solution.py:267
  21.6 0.0 collective-permute-start.7
  21.6 3.9 %collective-permute-done.4.rest_3_ = bf16[3,128,384]{2,1,0:T(8,128)(2,1)S(1)} collective-permute-done((bf16[3,128,384]{2,1,0:T(8,128)(2,1)}, bf16[3,128,384]{2,1,0:T(8,128)(2,1)S(1)}, u32[]{:S(2)}, u32[]{:S(2)}) %collective-permute-start.4) | collective-permute-done | bytes 294944 | tf_op jit(solution)/shard_map/ppermute | solution.py:267
  25.5 5.3 %collective-permute-start.8 = (bf16[3,128,384]{2,1,0:T(8,128)(2,1)S(1)}, bf16[3,128,384]{2,1,0:T(8,128)(2,1)S(1)}, u32[]{:S(2)}, u32[]{:S(2)}) collective-permute-start(bf16[3,128,384]{2,1,0:T(8,128)(2,1)S(1)} %collective-permute-done.4.rest_3_), channel_id=1, source_target_pairs={{0,1},{1,0},{2,3},{3,2},{4,5},{5,4},{6,7},{7,6},{8,9},{9,8},{10,11... | collective-permute-start | bytes 884744 | tf_op jit(solution)/shard_map/ppermute | solution.py:222
  30.8 0.0 collective-permute-done.1.rest_0_
  30.8 0.0 collective-permute-start.5
  30.8 0.0 collective-permute-done.other_w
  30.8 0.0 collective-permute-done.6.rest_5_
  30.8 0.0 collective-permute-done.7.rest_6_
  30.8 1.2 %collective-permute-done.8.rest_7_ = bf16[3,128,384]{2,1,0:T(8,128)(2,1)S(1)} collective-permute-done((bf16[3,128,384]{2,1,0:T(8,128)(2,1)S(1)}, bf16[3,128,384]{2,1,0:T(8,128)(2,1)S(1)}, u32[]{:S(2)}, u32[]{:S(2)}) %collective-permute-start.8) | collective-permute-done | bytes 294944 | tf_op jit(solution)/shard_map/ppermute | solution.py:222
  32.0 0.4 collective-permute-done.5.rest_4_
  32.4 1.6 %attend.2 = (bf16[64,384]{1,0:T(8,128)(2,1)S(1)}, bf16[64,384]{1,0:T(8,128)(2,1)S(1)}, bf16[64,384]{1,0:T(8,128)(2,1)S(1)}, bf16[64,384]{1,0:T(8,128)(2,1)S(1)}) custom-call(f32[512,1024]{1,0:T(8,128)S(1)} %bias.1.bias_ref, bf16[3,128,384]{2,1,0:T(8,128)(2,1)S(1)} %collective-permute-done.1.rest_0_, bf16[3,128,384]{2,1,0:T(8,128)(2,1)S(1)} %collective-permute-done.2.rest_1_, ...), custom_call_target="tpu_custom_call" | custom-call | tf_op jit(solution)/shard_map/attend/pallas_call | solution.py:277
  34.1 3.9 %collective-permute-start.9 = (bf16[64,384]{1,0:T(8,128)(2,1)S(1)}, bf16[64,384]{1,0:T(8,128)(2,1)S(1)}, u32[]{:S(2)}, u32[]{:S(2)}) collective-permute-start(bf16[64,384]{1,0:T(8,128)(2,1)S(1)} %get-tuple-element.34), channel_id=1, source_target_pairs={{0,4},{4,0},{8,12},{12,8},{1,5},{5,1},{9,13},{13,9},{2,6},{6,2},{1... | collective-permute-start | bytes 147464 | tf_op jit(solution)/shard_map/ppermute | solution.py:292
  38.0 0.0 collective-permute-start.10
  38.0 2.4 %collective-permute-start.11 = (bf16[64,384]{1,0:T(8,128)(2,1)S(1)}, bf16[64,384]{1,0:T(8,128)(2,1)S(1)}, u32[]{:S(2)}, u32[]{:S(2)}) collective-permute-start(bf16[64,384]{1,0:T(8,128)(2,1)S(1)} %get-tuple-element.36), channel_id=1, source_target_pairs={{0,12},{4,8},{8,4},{12,0},{1,13},{5,9},{9,5},{13,1},{2,14},{6,10},... | collective-permute-start | bytes 147464 | tf_op jit(solution)/shard_map/ppermute | solution.py:292
  40.4 1.6 %attend.3 = (bf16[64,384]{1,0:T(8,128)(2,1)S(1)}, bf16[64,384]{1,0:T(8,128)(2,1)S(1)}, bf16[64,384]{1,0:T(8,128)(2,1)S(1)}, bf16[64,384]{1,0:T(8,128)(2,1)S(1)}) custom-call(f32[512,1024]{1,0:T(8,128)S(1)} %bias.1.bias_ref, bf16[3,128,384]{2,1,0:T(8,128)(2,1)S(1)} %collective-permute-done.1.rest_0_, bf16[3,128,384]{2,1,0:T(8,128)(2,1)S(1)} %collective-permute-done.2.rest_1_, ...), custom_call_target="tpu_custom_call" | custom-call | tf_op jit(solution)/shard_map/attend/pallas_call | solution.py:277
  42.1 1.1 %collective-permute-start.13 = (bf16[64,384]{1,0:T(8,128)(2,1)S(1)}, bf16[64,384]{1,0:T(8,128)(2,1)S(1)}, u32[]{:S(2)}, u32[]{:S(2)}) collective-permute-start(bf16[64,384]{1,0:T(8,128)(2,1)S(1)} %get-tuple-element.40), channel_id=1, source_target_pairs={{0,4},{4,0},{8,12},{12,8},{1,5},{5,1},{9,13},{13,9},{2,6},{6,2},{1... | collective-permute-start | bytes 147464 | tf_op jit(solution)/shard_map/ppermute | solution.py:292
  43.2 0.9 %collective-permute-start.14 = (bf16[64,384]{1,0:T(8,128)(2,1)S(1)}, bf16[64,384]{1,0:T(8,128)(2,1)S(1)}, u32[]{:S(2)}, u32[]{:S(2)}) collective-permute-start(bf16[64,384]{1,0:T(8,128)(2,1)S(1)} %get-tuple-element.41), channel_id=1, source_target_pairs={{0,8},{4,12},{8,0},{12,4},{1,9},{5,13},{9,1},{13,5},{2,10},{6,14},... | collective-permute-start | bytes 147464 | tf_op jit(solution)/shard_map/ppermute | solution.py:292
  44.1 0.0 collective-permute-done.9.rest_1_
  44.1 2.4 %collective-permute-start.15 = (bf16[64,384]{1,0:T(8,128)(2,1)S(1)}, bf16[64,384]{1,0:T(8,128)(2,1)S(1)}, u32[]{:S(2)}, u32[]{:S(2)}) collective-permute-start(bf16[64,384]{1,0:T(8,128)(2,1)S(1)} %get-tuple-element.42), channel_id=1, source_target_pairs={{0,12},{4,8},{8,4},{12,0},{1,13},{5,9},{9,5},{13,1},{2,14},{6,10},... | collective-permute-start | bytes 147464 | tf_op jit(solution)/shard_map/ppermute | solution.py:292
  46.5 0.0 collective-permute-done.10.rest_2_
  46.5 0.0 collective-permute-done.11.rest_3_
  46.5 0.0 slice-done
  46.5 0.0 slice-done.1
  46.6 1.8 %project.2 = (f32[32,3072]{1,0:T(8,128)S(1)}, bf16[32,3072]{1,0:T(8,128)(2,1)S(1)}) custom-call(bf16[768,3072]{1,0:T(8,128)(2,1)S(1)} %bitcast.1, bf16[768,3072]{1,0:T(8,128)(2,1)S(1)} %collective-permute-done.other_w, bf16[64,384]{1,0:T(8,128)(2,1)S(1)} %get-tuple-element.33.rest_0_, bf16[64,384]{1,0:T(8,128)(2,1)S(1)} %collective-permute-done.9.rest_1_, ...), custom_call_target="tpu_custom_call" | custom-call | tf_op jit(solution)/shard_map/project/pallas_call | solution.py:294
  48.4 1.5 %collective-permute-start.12 = (bf16[32,3072]{1,0:T(8,128)(2,1)S(1)}, bf16[32,3072]{1,0:T(8,128)(2,1)S(1)}, u32[]{:S(2)}, u32[]{:S(2)}) collective-permute-start(bf16[32,3072]{1,0:T(8,128)(2,1)S(1)} %get-tuple-element.38), channel_id=1, source_target_pairs={{0,2},{2,0},{1,3},{3,1},{4,6},{6,4},{5,7},{7,5},{8,10},{10,8},{9,1... | collective-permute-start | bytes 589832 | tf_op jit(solution)/shard_map/ppermute | solution.py:222
  49.9 0.0 collective-permute-done.13.rest_1_
  49.9 0.0 collective-permute-done.14.rest_2_
  49.9 0.2 collective-permute-done.15.rest_3_
  50.1 1.8 %project.3 = (f32[32,3072]{1,0:T(8,128)S(1)}, bf16[32,3072]{1,0:T(8,128)(2,1)S(1)}) custom-call(bf16[768,3072]{1,0:T(8,128)(2,1)S(1)} %bitcast.1, bf16[768,3072]{1,0:T(8,128)(2,1)S(1)} %collective-permute-done.other_w, bf16[64,384]{1,0:T(8,128)(2,1)S(1)} %get-tuple-element.39.rest_0_, bf16[64,384]{1,0:T(8,128)(2,1)S(1)} %collective-permute-done.13.rest_1_, ...), custom_call_target="tpu_custom_call" | custom-call | tf_op jit(solution)/shard_map/project/pallas_call | solution.py:294
  51.9 1.5 %collective-permute-start.16 = (bf16[32,3072]{1,0:T(8,128)(2,1)S(1)}, bf16[32,3072]{1,0:T(8,128)(2,1)S(1)}, u32[]{:S(2)}, u32[]{:S(2)}) collective-permute-start(bf16[32,3072]{1,0:T(8,128)(2,1)S(1)} %get-tuple-element.44), channel_id=1, source_target_pairs={{0,2},{2,0},{1,3},{3,1},{4,6},{6,4},{5,7},{7,5},{8,10},{10,8},{9,1... | collective-permute-start | bytes 589832 | tf_op jit(solution)/shard_map/ppermute | solution.py:222
  53.4 1.9 %collective-permute-done.12.refs_1_ = bf16[32,3072]{1,0:T(8,128)(2,1)S(1)} collective-permute-done((bf16[32,3072]{1,0:T(8,128)(2,1)S(1)}, bf16[32,3072]{1,0:T(8,128)(2,1)S(1)}, u32[]{:S(2)}, u32[]{:S(2)}) %collective-permute-start.12) | collective-permute-done | bytes 196640 | tf_op jit(solution)/shard_map/ppermute | solution.py:222
  55.4 2.9 %collective-permute-done.16.refs_3_ = bf16[32,3072]{1,0:T(8,128)(2,1)S(1)} collective-permute-done((bf16[32,3072]{1,0:T(8,128)(2,1)S(1)}, bf16[32,3072]{1,0:T(8,128)(2,1)S(1)}, u32[]{:S(2)}, u32[]{:S(2)}) %collective-permute-start.16) | collective-permute-done | bytes 196640 | tf_op jit(solution)/shard_map/ppermute | solution.py:222
  58.3 0.8 %add.1 = bf16[1,64,3072]{2,1,0:T(8,128)(2,1)} custom-call(f32[32,3072]{1,0:T(8,128)S(1)} %get-tuple-element.37.refs_0_, bf16[32,3072]{1,0:T(8,128)(2,1)S(1)} %collective-permute-done.12.refs_1_, f32[32,3072]{1,0:T(8,128)S(1)} %get-tuple-element.43.refs_2_, bf16[32,3072]{1,0:T(8,128)(2,1)S(1)} %collective-permute-done.16.refs_3_), custom_call_target="tpu_custom_call" | custom-call | tf_op jit(solution)/shard_map/add/pallas_call | solution.py:307
  (1 shorter events, 0.0 us)
Async XLA Ops:
  2.4 28.4 %collective-permute-start = (bf16[768,3072]{1,0:T(8,128)(2,1)}, bf16[768,3072]{1,0:T(8,128)(2,1)S(1)}, u32[]{:S(2)}, u32[]{:S(2)}) collective-permute-start(bf16[768,3072]{1,0:T(8,128)(2,1)} %own_w.3), channel_id=1, source_target_pairs={{0,1},{1,0},{2,3},{3,2},{4,5},{5,4},{6,7},{7,6},{8,9},{9,8},{10,11... | collective-permute-start | bytes 14155784 | tf_op jit(solution)/shard_map/ppermute | solution.py:222
  2.9 10.8 %collective-permute-start.2 = (bf16[3,128,384]{2,1,0:T(8,128)(2,1)}, bf16[3,128,384]{2,1,0:T(8,128)(2,1)S(1)}, u32[]{:S(2)}, u32[]{:S(2)}) collective-permute-start(bf16[3,128,384]{2,1,0:T(8,128)(2,1)} %get-tuple-element.30), channel_id=1, source_target_pairs={{0,1},{1,9},{4,0},{5,8},{8,5},{9,13},{12,4},{13,12},{2,3},{3,11},{... | collective-permute-start | bytes 884744 | tf_op jit(solution)/shard_map/ppermute | solution.py:267
  3.0 18.6 %collective-permute-start.3 = (bf16[3,128,384]{2,1,0:T(8,128)(2,1)}, bf16[3,128,384]{2,1,0:T(8,128)(2,1)S(1)}, u32[]{:S(2)}, u32[]{:S(2)}) collective-permute-start(bf16[3,128,384]{2,1,0:T(8,128)(2,1)} %get-tuple-element.31), channel_id=1, source_target_pairs={{0,4},{1,12},{4,5},{5,13},{8,0},{9,8},{12,1},{13,9},{2,6},{3,14},{... | collective-permute-start | bytes 884744 | tf_op jit(solution)/shard_map/ppermute | solution.py:267
  5.6 19.9 %collective-permute-start.4 = (bf16[3,128,384]{2,1,0:T(8,128)(2,1)}, bf16[3,128,384]{2,1,0:T(8,128)(2,1)S(1)}, u32[]{:S(2)}, u32[]{:S(2)}) collective-permute-start(bf16[3,128,384]{2,1,0:T(8,128)(2,1)} %get-tuple-element.32), channel_id=1, source_target_pairs={{0,5},{1,13},{4,4},{5,12},{8,1},{9,9},{12,0},{13,8},{2,7},{3,15},{... | collective-permute-start | bytes 884744 | tf_op jit(solution)/shard_map/ppermute | solution.py:267
  9.9 0.7 %copy-start = (s32[4,4]{1,0:T(4,128)S(1)}, s32[4,4]{1,0:T(4,128)}, u32[]{:S(2)}) copy-start(s32[4,4]{1,0:T(4,128)} %band_ref.1) | copy-start | bytes 196
  10.6 0.7 %copy-start.1 = (s32[7]{0:T(128)S(1)}, s32[7]{0:T(128)}, u32[]{:S(2)}) copy-start(s32[7]{0:T(128)} %reach_ref.1) | copy-start | bytes 88
  11.2 35.3 %slice-start = ((s8[4718592]{0:T(1024)(128)(4,1)}), s8[4194304]{0:T(1024)(128)(4,1)S(1)}, s32[]{:S(2)}) async-start(s8[4718592]{0:T(1024)(128)(4,1)} %bitcast), calls=%async_computation | async-start | bytes 8388608
  12.0 34.6 %slice-start.1 = ((s8[4718592]{0:T(1024)(128)(4,1)}), s8[524288]{0:T(1024)(128)(4,1)S(1)}, s32[]{:S(2)}) async-start(s8[4718592]{0:T(1024)(128)(4,1)} %bitcast), calls=%async_computation.1 | async-start | bytes 1048576
  12.0 18.8 %collective-permute-start.1 = (bf16[3,128,384]{2,1,0:T(8,128)(2,1)}, bf16[3,128,384]{2,1,0:T(8,128)(2,1)S(1)}, u32[]{:S(2)}, u32[]{:S(2)}) collective-permute-start(bf16[3,128,384]{2,1,0:T(8,128)(2,1)} %get-tuple-element.29), channel_id=1, source_target_pairs={{0,0},{1,8},{4,1},{5,9},{8,4},{9,12},{12,5},{13,13},{2,2},{3,10},{... | collective-permute-start | bytes 884744 | tf_op jit(solution)/shard_map/ppermute | solution.py:267
  13.8 17.1 %collective-permute-start.6 = (bf16[3,128,384]{2,1,0:T(8,128)(2,1)S(1)}, bf16[3,128,384]{2,1,0:T(8,128)(2,1)S(1)}, u32[]{:S(2)}, u32[]{:S(2)}) collective-permute-start(bf16[3,128,384]{2,1,0:T(8,128)(2,1)S(1)} %collective-permute-done.2.rest_1_), channel_id=1, source_target_pairs={{0,1},{1,0},{2,3},{3,2},{4,5},{5,4},{6,7},{7,6},{8,9},{9,8},{10,11... | collective-permute-start | bytes 884744 | tf_op jit(solution)/shard_map/ppermute | solution.py:222
  21.6 9.2 %collective-permute-start.7 = (bf16[3,128,384]{2,1,0:T(8,128)(2,1)S(1)}, bf16[3,128,384]{2,1,0:T(8,128)(2,1)S(1)}, u32[]{:S(2)}, u32[]{:S(2)}) collective-permute-start(bf16[3,128,384]{2,1,0:T(8,128)(2,1)S(1)} %collective-permute-done.3.rest_2_), channel_id=1, source_target_pairs={{0,1},{1,0},{2,3},{3,2},{4,5},{5,4},{6,7},{7,6},{8,9},{9,8},{10,11... | collective-permute-start | bytes 884744 | tf_op jit(solution)/shard_map/ppermute | solution.py:222
  25.5 6.5 %collective-permute-start.8 = (bf16[3,128,384]{2,1,0:T(8,128)(2,1)S(1)}, bf16[3,128,384]{2,1,0:T(8,128)(2,1)S(1)}, u32[]{:S(2)}, u32[]{:S(2)}) collective-permute-start(bf16[3,128,384]{2,1,0:T(8,128)(2,1)S(1)} %collective-permute-done.4.rest_3_), channel_id=1, source_target_pairs={{0,1},{1,0},{2,3},{3,2},{4,5},{5,4},{6,7},{7,6},{8,9},{9,8},{10,11... | collective-permute-start | bytes 884744 | tf_op jit(solution)/shard_map/ppermute | solution.py:222
  30.8 1.6 %collective-permute-start.5 = (bf16[3,128,384]{2,1,0:T(8,128)(2,1)S(1)}, bf16[3,128,384]{2,1,0:T(8,128)(2,1)S(1)}, u32[]{:S(2)}, u32[]{:S(2)}) collective-permute-start(bf16[3,128,384]{2,1,0:T(8,128)(2,1)S(1)} %collective-permute-done.1.rest_0_), channel_id=1, source_target_pairs={{0,1},{1,0},{2,3},{3,2},{4,5},{5,4},{6,7},{7,6},{8,9},{9,8},{10,11... | collective-permute-start | bytes 884744 | tf_op jit(solution)/shard_map/ppermute | solution.py:222
  34.1 10.0 %collective-permute-start.9 = (bf16[64,384]{1,0:T(8,128)(2,1)S(1)}, bf16[64,384]{1,0:T(8,128)(2,1)S(1)}, u32[]{:S(2)}, u32[]{:S(2)}) collective-permute-start(bf16[64,384]{1,0:T(8,128)(2,1)S(1)} %get-tuple-element.34), channel_id=1, source_target_pairs={{0,4},{4,0},{8,12},{12,8},{1,5},{5,1},{9,13},{13,9},{2,6},{6,2},{1... | collective-permute-start | bytes 147464 | tf_op jit(solution)/shard_map/ppermute | solution.py:292
  38.0 8.5 %collective-permute-start.10 = (bf16[64,384]{1,0:T(8,128)(2,1)S(1)}, bf16[64,384]{1,0:T(8,128)(2,1)S(1)}, u32[]{:S(2)}, u32[]{:S(2)}) collective-permute-start(bf16[64,384]{1,0:T(8,128)(2,1)S(1)} %get-tuple-element.35), channel_id=1, source_target_pairs={{0,8},{4,12},{8,0},{12,4},{1,9},{5,13},{9,1},{13,5},{2,10},{6,14},... | collective-permute-start | bytes 147464 | tf_op jit(solution)/shard_map/ppermute | solution.py:292
  38.0 8.5 %collective-permute-start.11 = (bf16[64,384]{1,0:T(8,128)(2,1)S(1)}, bf16[64,384]{1,0:T(8,128)(2,1)S(1)}, u32[]{:S(2)}, u32[]{:S(2)}) collective-permute-start(bf16[64,384]{1,0:T(8,128)(2,1)S(1)} %get-tuple-element.36), channel_id=1, source_target_pairs={{0,12},{4,8},{8,4},{12,0},{1,13},{5,9},{9,5},{13,1},{2,14},{6,10},... | collective-permute-start | bytes 147464 | tf_op jit(solution)/shard_map/ppermute | solution.py:292
  42.1 7.8 %collective-permute-start.13 = (bf16[64,384]{1,0:T(8,128)(2,1)S(1)}, bf16[64,384]{1,0:T(8,128)(2,1)S(1)}, u32[]{:S(2)}, u32[]{:S(2)}) collective-permute-start(bf16[64,384]{1,0:T(8,128)(2,1)S(1)} %get-tuple-element.40), channel_id=1, source_target_pairs={{0,4},{4,0},{8,12},{12,8},{1,5},{5,1},{9,13},{13,9},{2,6},{6,2},{1... | collective-permute-start | bytes 147464 | tf_op jit(solution)/shard_map/ppermute | solution.py:292
  43.2 6.7 %collective-permute-start.14 = (bf16[64,384]{1,0:T(8,128)(2,1)S(1)}, bf16[64,384]{1,0:T(8,128)(2,1)S(1)}, u32[]{:S(2)}, u32[]{:S(2)}) collective-permute-start(bf16[64,384]{1,0:T(8,128)(2,1)S(1)} %get-tuple-element.41), channel_id=1, source_target_pairs={{0,8},{4,12},{8,0},{12,4},{1,9},{5,13},{9,1},{13,5},{2,10},{6,14},... | collective-permute-start | bytes 147464 | tf_op jit(solution)/shard_map/ppermute | solution.py:292
  44.1 6.0 %collective-permute-start.15 = (bf16[64,384]{1,0:T(8,128)(2,1)S(1)}, bf16[64,384]{1,0:T(8,128)(2,1)S(1)}, u32[]{:S(2)}, u32[]{:S(2)}) collective-permute-start(bf16[64,384]{1,0:T(8,128)(2,1)S(1)} %get-tuple-element.42), channel_id=1, source_target_pairs={{0,12},{4,8},{8,4},{12,0},{1,13},{5,9},{9,5},{13,1},{2,14},{6,10},... | collective-permute-start | bytes 147464 | tf_op jit(solution)/shard_map/ppermute | solution.py:292
  48.4 7.0 %collective-permute-start.12 = (bf16[32,3072]{1,0:T(8,128)(2,1)S(1)}, bf16[32,3072]{1,0:T(8,128)(2,1)S(1)}, u32[]{:S(2)}, u32[]{:S(2)}) collective-permute-start(bf16[32,3072]{1,0:T(8,128)(2,1)S(1)} %get-tuple-element.38), channel_id=1, source_target_pairs={{0,2},{2,0},{1,3},{3,1},{4,6},{6,4},{5,7},{7,5},{8,10},{10,8},{9,1... | collective-permute-start | bytes 589832 | tf_op jit(solution)/shard_map/ppermute | solution.py:222
  51.9 6.4 %collective-permute-start.16 = (bf16[32,3072]{1,0:T(8,128)(2,1)S(1)}, bf16[32,3072]{1,0:T(8,128)(2,1)S(1)}, u32[]{:S(2)}, u32[]{:S(2)}) collective-permute-start(bf16[32,3072]{1,0:T(8,128)(2,1)S(1)} %get-tuple-element.44), channel_id=1, source_target_pairs={{0,2},{2,0},{1,3},{3,1},{4,6},{6,4},{5,7},{7,5},{8,10},{10,8},{9,1... | collective-permute-start | bytes 589832 | tf_op jit(solution)/shard_map/ppermute | solution.py:222
